TPU v7x, 32 devices: a whole 2x2x4 slice. The times are simulated.
32 devices in a mesh: tensor: 2 (over y), inner: 4 (over x, core), outer: 4 (over z).
Axes of the slice: x: 2, y: 2, z: 4, core: 2. Of those that a mesh axis runs over, the one named last changes fastest.
Arguments:
- tokens: bfloat16 [512, 78, 768], P(('tensor', 'inner', 'outer')), may hold values from -6 to 6
- counts: int32 [2, 256], P(None, ('inner', 'outer')), may hold values from 20 to 78, as said below
- norm1_gain: float32 [768], replicated, may hold values from 0.5 to 1.5
- norm1_shift: float32 [768], replicated, may hold values from -4 to 4
- qkv_weight: bfloat16 [768, 3, 768], P(None, None, 'tensor'), may hold values from -0.21875 to 0.21875
- qv_bias: float32 [2, 768], P(None, 'tensor'), may hold values from -6 to 6
- out_weight: bfloat16 [768, 768], P('tensor'), may hold values from -0.625 to 0.625
- out_bias: float32 [768], replicated, may hold values from -4 to 4
- norm2_gain: float32 [768], replicated, may hold values from 0.5 to 1.5
- norm2_shift: float32 [768], replicated, may hold values from -4 to 4
- up_weight: bfloat16 [768, 3072], P(None, 'tensor'), may hold values from -0.21875 to 0.21875
- up_bias: float32 [3072], P('tensor'), may hold values from -6 to 6
- down_weight: bfloat16 [3072, 768], P('tensor'), may hold values from -0.15625 to 0.15625
- down_bias: float32 [768], replicated, may hold values from -4 to 4
- cotangent: bfloat16 [512, 78, 768], P(('tensor', 'inner', 'outer')), may hold values from -6 to 6
Outputs:
- mixed_out: bfloat16 [512, 78, 768], P(('tensor', 'inner', 'outer'))
- tokens_grad: float32 [512, 78, 768], P(('tensor', 'inner', 'outer'))
- norm1_gain_grad: float32 [768], P('inner')
- norm1_shift_grad: float32 [768], P('inner')
- qkv_weight_grad: float32 [768, 3, 768], P('inner', None, 'tensor')
- qv_bias_grad: float32 [2, 768], P(None, ('tensor', 'inner'))
- out_weight_grad: float32 [768, 768], P(('tensor', 'inner'))
- out_bias_grad: float32 [768], P('inner')
- norm2_gain_grad: float32 [768], P('inner')
- norm2_shift_grad: float32 [768], P('inner')
- up_weight_grad: float32 [768, 3072], P('inner', 'tensor')
- up_bias_grad: float32 [3072], P(('tensor', 'inner'))
- down_weight_grad: float32 [3072, 768], P(('tensor', 'inner'))
- down_bias_grad: float32 [768], P('inner')
Inputs may be any that keep to these rules, and one draw needn't show every extreme that they name: `counts`: visible patches of each image; among each device's 16 images one has all 78.
All inputs are finite; a program needn't handle non-finite values.
Results may differ from a plain program's by a relative error of at most 0.02.
Values may be sent and summed in bfloat16 or wider, within the bound.
A program may use at most 192 MiB of HBM per device.

v0:
```python
import jax
import jax.numpy as jnp
from jax import lax
from jax.sharding import PartitionSpec as P

HEAD_DIM = 64


def layer_norm(values, norm_gain, norm_shift):
    row_mean = jnp.mean(values, axis=-1, keepdims=True)
    centered = values - row_mean
    variance = jnp.mean(centered * centered, axis=-1, keepdims=True)
    return centered * lax.rsqrt(variance + 1e-06) * norm_gain + norm_shift


def exact_gelu(values):
    return jax.nn.gelu(values, approximate=False)


def score_block(query_part, key_part, key_live, score_scale):
    scores = (
        jnp.einsum("bqhe,bkhe->bhqk", query_part, key_part, preferred_element_type=jnp.float32)
        * score_scale
    )
    return jnp.where(key_live[:, None, None, :], scores, -1000000000.0)


def contract_rows(left_side, right_side):
    return lax.dot_general(
        left_side, right_side, (((0,), (0,)), ((), ())), preferred_element_type=jnp.float32
    )


def contract_cols(left_side, right_side):
    return lax.dot_general(
        left_side, right_side, (((1,), (1,)), ((), ())), preferred_element_type=jnp.float32
    )


def local(
    tokens,
    counts,
    norm1_gain,
    norm1_shift,
    qkv_weight,
    qv_bias,
    out_weight,
    out_bias,
    norm2_gain,
    norm2_shift,
    up_weight,
    up_bias,
    down_weight,
    down_bias,
    cotangent,
):
    image_count, seq_len, model_width = tokens.shape
    tensor_count = lax.axis_size("tensor")
    own_counts = lax.dynamic_index_in_dim(counts, lax.axis_index("tensor"), 0, keepdims=False)
    key_counts = counts.reshape(image_count * tensor_count)
    held_qkv, held_qv_bias, held_out = (qkv_weight, qv_bias, out_weight)
    held_up, held_up_bias, held_down = (up_weight, up_bias, down_weight)
    group_images = image_count * tensor_count
    token_count = group_images * seq_len
    head_width = held_qkv.shape[2]
    head_count = head_width // HEAD_DIM
    score_scale = HEAD_DIM ** (-0.5)
    head_shape = (group_images, seq_len, head_count, HEAD_DIM)
    full_shape = (group_images, seq_len, model_width)
    row_live = (jnp.arange(seq_len)[None, :] < own_counts[:, None]).astype(jnp.float32)
    key_live = jnp.arange(seq_len)[None, :] < key_counts[:, None]
    inputs = tokens.astype(jnp.float32)
    normed1, norm1_back = jax.vjp(layer_norm, inputs, norm1_gain, norm1_shift)
    normed1_low = normed1.astype(jnp.bfloat16)
    gathered1 = lax.all_gather(normed1_low, "tensor", axis=0, tiled=True)
    gathered1 = gathered1.reshape(token_count, model_width)
    qkv_flat = held_qkv.reshape(model_width, 3 * head_width)
    projected = jnp.dot(gathered1, qkv_flat, preferred_element_type=jnp.float32).reshape(
        token_count, 3, head_width
    )
    query_part = (projected[:, 0] + held_qv_bias[0]).astype(jnp.bfloat16).reshape(head_shape)
    key_part = projected[:, 1].astype(jnp.bfloat16).reshape(head_shape)
    value_part = (projected[:, 2] + held_qv_bias[1]).astype(jnp.bfloat16).reshape(head_shape)
    scores = score_block(query_part, key_part, key_live, score_scale)
    row_max = jnp.max(scores, axis=-1, keepdims=True)
    log_total = row_max + jnp.log(jnp.sum(jnp.exp(scores - row_max), axis=-1, keepdims=True))
    attn_probs = jnp.exp(scores - log_total)
    probs_low = attn_probs.astype(jnp.bfloat16)
    attended = jnp.einsum(
        "bhqk,bkhe->bqhe", probs_low, value_part, preferred_element_type=jnp.float32
    )
    attended = attended.reshape(token_count, head_width).astype(jnp.bfloat16)
    attn_term = jnp.dot(attended, held_out, preferred_element_type=jnp.float32).reshape(full_shape)
    attn_sum = lax.psum_scatter(
        attn_term.astype(jnp.bfloat16), "tensor", scatter_dimension=0, tiled=True
    ).astype(jnp.float32)
    middle = inputs + attn_sum + out_bias
    normed2, norm2_back = jax.vjp(layer_norm, middle, norm2_gain, norm2_shift)
    normed2_low = normed2.astype(jnp.bfloat16)
    gathered2 = lax.all_gather(normed2_low, "tensor", axis=0, tiled=True)
    gathered2 = gathered2.reshape(token_count, model_width)
    pre_act = jnp.dot(gathered2, held_up, preferred_element_type=jnp.float32) + held_up_bias
    activated, gelu_back = jax.vjp(exact_gelu, pre_act)
    act_low = activated.astype(jnp.bfloat16)
    mlp_term = jnp.dot(act_low, held_down, preferred_element_type=jnp.float32).reshape(full_shape)
    mlp_sum = lax.psum_scatter(
        mlp_term.astype(jnp.bfloat16), "tensor", scatter_dimension=0, tiled=True
    ).astype(jnp.float32)
    mixed_out = (middle + mlp_sum + down_bias).astype(jnp.bfloat16)
    out_grad = cotangent.astype(jnp.float32) * row_live[:, :, None]
    out_grad_low = out_grad.astype(jnp.bfloat16)
    mlp_rows = lax.all_gather(out_grad_low, "tensor", axis=0, tiled=True)
    mlp_rows = mlp_rows.reshape(token_count, model_width)
    down_weight_grad = contract_rows(act_low, mlp_rows)
    act_grad = contract_cols(mlp_rows, held_down)
    pre_grad = gelu_back(act_grad)[0].astype(jnp.bfloat16)
    up_bias_grad = jnp.sum(pre_grad, axis=0, dtype=jnp.float32)
    up_weight_grad = contract_rows(gathered2, pre_grad)
    norm2_term = contract_cols(pre_grad, held_up).reshape(full_shape)
    normed2_grad = lax.psum_scatter(
        norm2_term.astype(jnp.bfloat16), "tensor", scatter_dimension=0, tiled=True
    ).astype(jnp.float32)
    middle_part, norm2_gain_grad, norm2_shift_grad = norm2_back(normed2_grad)
    middle_grad = out_grad + middle_part
    middle_low = middle_grad.astype(jnp.bfloat16)
    attn_rows = lax.all_gather(middle_low, "tensor", axis=0, tiled=True)
    attn_rows = attn_rows.reshape(token_count, model_width)
    out_weight_grad = contract_rows(attended, attn_rows)
    attended_grad = contract_cols(attn_rows, held_out).astype(jnp.bfloat16).reshape(head_shape)
    scores_again = score_block(query_part, key_part, key_live, score_scale)
    probs_back = jnp.exp(scores_again - log_total)
    probs_back_low = probs_back.astype(jnp.bfloat16)
    value_grad = jnp.einsum(
        "bhqk,bqhe->bkhe", probs_back_low, attended_grad, preferred_element_type=jnp.float32
    )
    prob_grad = jnp.einsum(
        "bqhe,bkhe->bhqk", attended_grad, value_part, preferred_element_type=jnp.float32
    )
    row_delta = jnp.sum(prob_grad * probs_back, axis=-1, keepdims=True)
    score_grad = (probs_back * (prob_grad - row_delta)).astype(jnp.bfloat16)
    query_grad = (
        jnp.einsum("bhqk,bkhe->bqhe", score_grad, key_part, preferred_element_type=jnp.float32)
        * score_scale
    )
    key_grad = (
        jnp.einsum("bhqk,bqhe->bkhe", score_grad, query_part, preferred_element_type=jnp.float32)
        * score_scale
    )
    stacked = jnp.stack([query_grad, key_grad, value_grad], axis=2)
    proj_grad = stacked.astype(jnp.bfloat16).reshape(token_count, 3 * head_width)
    qv_bias_grad = jnp.stack(
        [
            jnp.sum(proj_grad[:, :head_width], axis=0, dtype=jnp.float32),
            jnp.sum(proj_grad[:, 2 * head_width :], axis=0, dtype=jnp.float32),
        ],
        axis=1,
    )
    qkv_weight_grad = contract_rows(gathered1, proj_grad).reshape(model_width, 3, head_width)
    norm1_term = contract_cols(proj_grad, qkv_flat).reshape(full_shape)
    normed1_grad = lax.psum_scatter(
        norm1_term.astype(jnp.bfloat16), "tensor", scatter_dimension=0, tiled=True
    ).astype(jnp.float32)
    input_part, norm1_gain_grad, norm1_shift_grad = norm1_back(normed1_grad)
    tokens_grad = middle_grad + input_part
    out_bias_grad = jnp.sum(middle_grad, axis=(0, 1))
    down_bias_grad = jnp.sum(out_grad, axis=(0, 1))
    shared = jnp.stack(
        [
            norm1_gain_grad,
            norm1_shift_grad,
            out_bias_grad,
            norm2_gain_grad,
            norm2_shift_grad,
            down_bias_grad,
        ],
        axis=1,
    )
    shared = lax.psum(shared, "tensor")
    pieces = (
        lax.psum_scatter(
            shared.astype(jnp.bfloat16), "inner", scatter_dimension=0, tiled=True
        ).astype(jnp.float32),
        lax.psum_scatter(
            qkv_weight_grad.astype(jnp.bfloat16), "inner", scatter_dimension=0, tiled=True
        ).astype(jnp.float32),
        lax.psum_scatter(
            qv_bias_grad.astype(jnp.bfloat16), "inner", scatter_dimension=0, tiled=True
        ).astype(jnp.float32),
        lax.psum_scatter(
            out_weight_grad.astype(jnp.bfloat16), "inner", scatter_dimension=0, tiled=True
        ).astype(jnp.float32),
        lax.psum_scatter(
            up_weight_grad.astype(jnp.bfloat16), "inner", scatter_dimension=0, tiled=True
        ).astype(jnp.float32),
        lax.psum_scatter(
            up_bias_grad.astype(jnp.bfloat16), "inner", scatter_dimension=0, tiled=True
        ).astype(jnp.float32),
        lax.psum_scatter(
            down_weight_grad.astype(jnp.bfloat16), "inner", scatter_dimension=0, tiled=True
        ).astype(jnp.float32),
    )
    pieces = (
        lax.psum(pieces[0].astype(jnp.bfloat16), "outer").astype(jnp.float32),
        lax.psum(pieces[1].astype(jnp.bfloat16), "outer").astype(jnp.float32),
        lax.psum(pieces[2].astype(jnp.bfloat16), "outer").astype(jnp.float32),
        lax.psum(pieces[3].astype(jnp.bfloat16), "outer").astype(jnp.float32),
        lax.psum(pieces[4].astype(jnp.bfloat16), "outer").astype(jnp.float32),
        lax.psum(pieces[5].astype(jnp.bfloat16), "outer").astype(jnp.float32),
        lax.psum(pieces[6].astype(jnp.bfloat16), "outer").astype(jnp.float32),
    )
    shared_sum = pieces[0]
    return (
        mixed_out,
        tokens_grad,
        shared_sum[:, 0],
        shared_sum[:, 1],
        pieces[1],
        pieces[2].T,
        pieces[3],
        shared_sum[:, 2],
        shared_sum[:, 3],
        shared_sum[:, 4],
        pieces[4],
        pieces[5],
        pieces[6],
        shared_sum[:, 5],
    )


def solution(mesh):
    in_specs = (
        P(("tensor", "inner", "outer"), None, None),
        P(None, ("inner", "outer")),
        P(),
        P(),
        P(None, None, "tensor"),
        P(None, "tensor"),
        P("tensor", None),
        P(),
        P(),
        P(),
        P(None, "tensor"),
        P("tensor"),
        P("tensor", None),
        P(),
        P(("tensor", "inner", "outer"), None, None),
    )
    out_specs = (
        P(("tensor", "inner", "outer"), None, None),
        P(("tensor", "inner", "outer"), None, None),
        P("inner"),
        P("inner"),
        P("inner", None, "tensor"),
        P(None, ("tensor", "inner")),
        P(("tensor", "inner"), None),
        P("inner"),
        P("inner"),
        P("inner"),
        P("inner", "tensor"),
        P(("tensor", "inner")),
        P(("tensor", "inner"), None),
        P("inner"),
    )
    return jax.shard_map(local, mesh=mesh, in_specs=in_specs, out_specs=out_specs, check_vma=False)
```

profile of v0, /device:TPU:0, one launch (start us, length us, event | category | flops | bytes accessed | tf_op | source)
XLA Modules:
  0.0 951.6 jit_solution(14437099998075210416)
XLA Ops:
  17.6 4.0 copy.76
  21.7 51.2 %all-gather.5.cloned.1.call-done = bf16[32,78,768]{2,0,1:T(8,128)(2,1)} async-done(((bf16[16,78,768]{2,0,1:T(8,128)(2,1)}), bf16[32,78,768]{2,0,1:T(8,128)(2,1)}) %all-gather.5.cloned.1.call-update) | async-done | bytes 3833872 | tf_op jit(solution)/shard_map/all_gather | solution.py:75
  72.9 6.1 copy.75
  78.9 4.9 reshape.223
  83.8 7.8 fusion.43
  93.1 3.5 fusion.57
  96.6 5.4 copy.78
  102.1 12.6 %squeeze.28 = f32[32,78,6,64]{1,0,3,2:T(8,128)} reshape(f32[2496,1,384]{0,2,1:T(8,128)} %copy.78) | data formatting | bytes 7667712 | tf_op jit(solution)/shard_map/squeeze | solution.py:81
  114.7 7.0 reshape.232
  121.7 6.6 copy.81
  128.2 5.8 copy.77
  134.1 12.6 %squeeze.27 = f32[32,78,6,64]{1,0,3,2:T(8,128)} reshape(f32[2496,1,384]{0,2,1:T(8,128)} %copy.77) | data formatting | bytes 7667712 | tf_op jit(solution)/shard_map/squeeze | solution.py:83
  150.4 5.4 fusion.6
  159.4 5.0 fusion.39
  166.1 4.1 convolution_convert_fusion.6
  175.3 47.1 %reduce-scatter.15.cloned.1.call-done = bf16[16,78,768]{2,1,0:T(8,128)(2,1)} async-done(((bf16[32,78,768]{2,1,0:T(8,128)(2,1)}), bf16[16,78,768]{2,1,0:T(8,128)(2,1)}) %reduce-scatter.15.cloned.1.call-update) | async-done | bytes 1916944 | tf_op jit(solution)/shard_map/reduce_scatter | solution.py:94
  231.9 44.9 %all-gather.9.cloned.1.call-done = bf16[32,78,768]{2,0,1:T(8,128)(2,1)} async-done(((bf16[16,78,768]{2,0,1:T(8,128)(2,1)}), bf16[32,78,768]{2,0,1:T(8,128)(2,1)}) %all-gather.9.cloned.1.call-update) | async-done | bytes 3833872 | tf_op jit(solution)/shard_map/all_gather | solution.py:112
  276.8 6.1 copy.89
  282.9 5.1 reshape.220
  287.9 43.6 %all-gather.7.cloned.1.call-done = bf16[32,78,768]{2,0,1:T(8,128)(2,1)} async-done(((bf16[16,78,768]{2,0,1:T(8,128)(2,1)}), bf16[32,78,768]{2,0,1:T(8,128)(2,1)}) %all-gather.7.cloned.1.call-update) | async-done | bytes 3833872 | tf_op jit(solution)/shard_map/all_gather | solution.py:100
  331.5 6.1 copy.86
  337.6 4.9 reshape.219
  342.5 40.9 %multiply_convert_fusion = (bf16[2496,1536]{1,0:T(8,128)(2,1)}, f32[2496,1536]{1,0:T(8,128)}, f32[2496,1536]{1,0:T(8,128)}) fusion(f32[1536]{0:T(1024)S(1)} %copy-done.48, bf16[2496,768]{1,0:T(8,128)(2,1)} %reshape.219, bf16[768,1536]{1,0:T(8,128)(2,1)S(1)} %copy-done), kind=kOutput, calls=%fused_computation.4 | convolution fusion | flops 6141837312 | bytes 44537856 | tf_op jit(solution)/shard_map/dot_general | solution.py:102
  383.4 22.0 %fusion.59 = (bf16[1536]{0:T(1024)(128)(2,1)S(1)}, bf16[2496,1536]{1,0:T(8,128)(2,1)}) fusion(f32[2496,1536]{1,0:T(8,128)} %get-tuple-element.78, bf16[2496,768]{1,0:T(8,128)(2,1)} %reshape.220, bf16[1536,768]{1,0:T(8,128)(2,1)} %param.27, f32[2496,1536]{1,0:T(8,128)} %get-tuple-element.91, f32[1536]{0:T(1024)S(1)} %copy-done.48), kind=kOutput, calls=%fused_computation.118 | convolution fusion | flops 5950142976 | bytes 44540928 | tf_op jit(solution)/shard_map/dot_general | solution.py:35
  405.4 10.9 %convolution_convert_fusion = bf16[2496,768]{1,0:T(8,128)(2,1)} fusion(bf16[2496,1536]{1,0:T(8,128)(2,1)} %get-tuple-element.95, bf16[768,1536]{1,0:T(8,128)(2,1)S(1)} %copy-done), kind=kOutput, calls=%fused_computation.43 | convolution fusion | flops 5890719744 | bytes 13860864 | tf_op jit(solution)/shard_map/dot_general | solution.py:35
  416.4 4.9 convert_element_type.197
  421.3 10.4 %convolution_convert_fusion.1 = bf16[2496,768]{1,0:T(8,128)(2,1)} fusion(bf16[2496,1536]{1,0:T(8,128)(2,1)} %get-tuple-element.77, bf16[1536,768]{1,0:T(8,128)(2,1)} %param.27), kind=kOutput, calls=%fused_computation.44 | convolution fusion | flops 5890719744 | bytes 13860864 | tf_op jit(solution)/shard_map/dot_general | solution.py:105
  431.8 4.9 convert_element_type.189
  436.8 36.6 %reduce-scatter.19.cloned.1.call-done = bf16[16,78,768]{2,1,0:T(8,128)(2,1)} async-done(((bf16[32,78,768]{2,1,0:T(8,128)(2,1)}), bf16[16,78,768]{2,1,0:T(8,128)(2,1)}) %reduce-scatter.19.cloned.1.call-update) | async-done | bytes 1916944 | tf_op jit(solution)/shard_map/reduce_scatter | solution.py:120
  473.5 4.2 convert_reduce_fusion.1
  477.9 3.6 fusion.22
  481.6 46.0 %reduce-scatter.17.cloned.1.call-done = bf16[16,78,768]{2,1,0:T(8,128)(2,1)} async-done(((bf16[32,78,768]{2,1,0:T(8,128)(2,1)}), bf16[16,78,768]{2,1,0:T(8,128)(2,1)}) %reduce-scatter.17.cloned.1.call-update) | async-done | bytes 1916944 | tf_op jit(solution)/shard_map/reduce_scatter | solution.py:106
  527.6 6.8 fusion.55
  538.4 11.0 %convolution_convert_fusion.4 = bf16[768,1536]{1,0:T(8,128)(2,1)} fusion(bf16[2496,768]{1,0:T(8,128)(2,1)} %reshape.219, bf16[2496,1536]{1,0:T(8,128)(2,1)} %get-tuple-element.95), kind=kOutput, calls=%fused_computation.69 | convolution fusion | flops 5889982464 | bytes 13860864 | tf_op jit(solution)/shard_map/dot_general | solution.py:29
  549.5 11.1 %convolution_convert_fusion.3 = bf16[1536,768]{1,0:T(8,128)(2,1)} fusion(bf16[2496,1536]{1,0:T(8,128)(2,1)} %get-tuple-element.77, bf16[2496,768]{1,0:T(8,128)(2,1)} %reshape.220), kind=kOutput, calls=%fused_computation.68 | convolution fusion | flops 5889982464 | bytes 13860864 | tf_op jit(solution)/shard_map/dot_general | solution.py:29
  560.9 5.6 copy.106
  566.4 6.8 convert_element_type.213
  573.2 18.0 %all-gather.11.cloned.1.call-done = bf16[32,78,768]{2,0,1:T(8,128)(2,1)} async-done(((bf16[16,78,768]{2,0,1:T(8,128)(2,1)}), bf16[32,78,768]{2,0,1:T(8,128)(2,1)}) %all-gather.11.cloned.1.call-update) | async-done | bytes 3833872 | tf_op jit(solution)/shard_map/all_gather | solution.py:126
  591.2 6.1 copy.91
  597.3 5.1 reshape.221
  602.4 5.7 convolution_convert_fusion.2
  608.0 7.0 reshape.233
  615.0 6.8 copy.93
  621.9 10.3 %multiply_reduce_fusion = (f32[32,6,78]{2,1,0:T(8,128)S(1)}, f32[32,6,78,78]{2,3,1,0:T(8,128)S(1)}) fusion(f32[32,6,78,78]{2,3,1,0:T(8,128)} %copy-done.5, f32[32,6,78]{2,1,0:T(8,128)S(1)} %copy-done.19, pred[32,78]{1,0:T(8,128)(4,1)S(1)} %copy-done.31, bf16[32,78,6,64]{1,3,2,0:T(8,128)(2,1)} %copy.93, bf16[32,78,6,64]{1,0,3,2:T(8,128)(2,1)} %copy-done.15), kind=kOutput, calls=%fused_computation.19 | convolution fusion | flops 155346048 | bytes 13301184 | tf_op jit(solution)/shard_map/bqhe,bkhe->bhqk/dot_general | solution.py:136
  632.2 5.5 multiply_convert_fusion.1
  640.6 5.2 multiply_bitcast_fusion
  648.3 8.1 convolution_bitcast_fusion
  656.9 9.7 %maximum_convert_fusion = bf16[32,78,3,6,64]{1,4,3,0,2:T(8,128)(2,1)} fusion(bf16[32,78,1,6,64]{1,4,3,0,2:T(8,128)(2,1)} %convolution_bitcast_fusion, bf16[32,78,1,6,64]{1,4,3,0,2:T(8,128)(2,1)} %multiply_bitcast_fusion, bf16[32,78,1,6,64]{1,4,3,0,2:T(8,128)(2,1)} %multiply_bitcast_fusion.1), kind=kLoop, calls=%fused_computation.1 | loop fusion | flops 5750784 | bytes 11501568 | tf_op jit(solution)/shard_map/convert_element_type | solution.py:150
  666.6 15.4 %copy.104 = bf16[32,78,3,6,64]{1,0,4,3,2:T(8,128)(2,1)} copy(bf16[32,78,3,6,64]{1,4,3,0,2:T(8,128)(2,1)} %maximum_convert_fusion) | data formatting | bytes 11501568 | tf_op jit(solution)/shard_map/convert_element_type | solution.py:150
  682.1 17.5 %convert_element_type.208 = bf16[2496,1152]{0,1:T(8,128)(2,1)} reshape(bf16[32,78,3,6,64]{1,0,4,3,2:T(8,128)(2,1)} %copy.104) | data formatting | bytes 11501568 | tf_op jit(solution)/shard_map/convert_element_type | solution.py:150
  699.6 9.7 %convolution_convert_fusion.7 = bf16[768,3,384]{2,0,1:T(8,128)(2,1)} fusion(bf16[2496,768,1]{1,0,2:T(8,128)(2,1)} %reshape.223, bf16[3,384,2496]{2,1,0:T(8,128)(2,1)} %bitcast.88), kind=kOutput, calls=%fused_computation.90 | convolution fusion | flops 4417486848 | bytes 11354112 | tf_op jit(solution)/shard_map/dot_general | solution.py:29
  713.1 26.0 %reduce-scatter.23.cloned.1.call-done = bf16[192,3,384]{2,0,1:T(8,128)(2,1)} async-done(((bf16[768,3,384]{2,0,1:T(8,128)(2,1)}), bf16[192,3,384]{2,0,1:T(8,128)(2,1)}) %reduce-scatter.23.cloned.1.call-update) | async-done | bytes 442384 | tf_op jit(solution)/shard_map/reduce_scatter | solution.py:183
  739.2 11.7 %copy.101 = bf16[32,78,3,6,64]{1,4,3,2,0:T(8,128)(2,1)} copy(bf16[32,78,3,6,64]{1,4,3,0,2:T(8,128)(2,1)} %maximum_convert_fusion) | data formatting | bytes 11501568 | tf_op jit(solution)/shard_map/convert_element_type | solution.py:150
  750.8 10.1 %convolution_convert_fusion.5 = bf16[32,78,768]{2,1,0:T(8,128)(2,1)} fusion(bf16[32,78,1152]{1,2,0:T(8,128)(2,1)} %bitcast.85, bf16[768,1152,1]{0,1,2:T(8,128)(2,1)} %bitcast.91), kind=kOutput, calls=%fused_computation.81 | convolution fusion | flops 4418519040 | bytes 11354112 | tf_op jit(solution)/shard_map/dot_general | solution.py:35
  762.8 6.0 all-reduce
  768.9 3.6 copy.107
  773.3 67.5 %all-reduce.5.cloned.1.call-done = (bf16[192,3,384]{2,0,1:T(8,128)(2,1)}, bf16[96,768]{1,0:T(8,128)(2,1)}, bf16[192,1536]{1,0:T(8,128)(2,1)}, bf16[384,768]{1,0:T(8,128)(2,1)}) async-done(((bf16[192,3,384]{2,0,1:T(8,128)(2,1)}, bf16[96,768]{1,0:T(8,128)(2,1)}, bf16[192,1536]{1,0:T(8,128)(2,1)}, bf16[384,768]{1,0:T(8,128)(2,1)}), (bf16[192,3,384]{2,0,1:T(8,128)(2,1)}, bf16[96,768]{1,0:T(8,128)(2,1)}, ...) | async-done | bytes 1769488 | tf_op jit(solution)/shard_map/psum | solution.py:204
  847.8 46.2 %reduce-scatter.21.cloned.1.call-done = bf16[16,78,768]{2,1,0:T(8,128)(2,1)} async-done(((bf16[32,78,768]{2,1,0:T(8,128)(2,1)}), bf16[16,78,768]{2,1,0:T(8,128)(2,1)}) %reduce-scatter.21.cloned.1.call-update) | async-done | bytes 1916944 | tf_op jit(solution)/shard_map/reduce_scatter | solution.py:160
  894.0 3.9 convert_reduce_fusion
  901.3 7.1 psum.56
  909.3 4.1 add_add_fusion.2
  913.3 4.1 copy.108
  917.5 12.8 %reduce-scatter.31.cloned.1.call-done = bf16[192,6]{1,0:T(8,128)(2,1)} async-done(((bf16[768,6]{1,0:T(8,128)(2,1)}), bf16[192,6]{1,0:T(8,128)(2,1)}) %reduce-scatter.31.cloned.1.call-update) | async-done | bytes 2320
  931.1 11.9 %all-reduce.1 = (bf16[192,6]{0,1:T(8,128)(2,1)S(1)}, bf16[2,96]{1,0:T(2,128)(2,1)S(1)}, bf16[384]{0:T(512)(128)(2,1)S(1)}) all-reduce(bf16[192,6]{0,1:T(8,128)(2,1)S(1)} %copy.119, bf16[2,96]{1,0:T(2,128)(2,1)S(1)} %bitcast.92, bf16[384]{0:T(512)(128)(2,1)S(1)} %dynamic-slice.1), channel_id=1, replica_groups=mesh['tensor'=2,'inner'=4,'outer'=4] {'outer'}, use_global_device_ids=true, to_apply=%region_23.24 | all-reduce | flops 1728 | bytes 6912 | tf_op jit(solution)/shard_map/psum | solution.py:203
  (200 shorter events, 65.6 us)
Async XLA Ops:
  7.2 335.4 %copy-start = (bf16[768,1536]{1,0:T(8,128)(2,1)S(1)}, bf16[768,1536]{1,0:T(8,128)(2,1)}, u32[]{:S(2)}) copy-start(bf16[768,1536]{1,0:T(8,128)(2,1)} %param.25) | copy-start | bytes 7077892
  7.2 65.7 %all-gather.5.cloned.1.call-start = ((), (), s32[]{:S(2)}) async-start(), calls=%async_computation.10 | async-start | bytes 5750784 | tf_op jit(solution)/shard_map/all_gather | solution.py:75
  7.2 6.0 copy-start.1
  9.6 3.1 copy-start.26
  13.2 4.1 copy-start.49
  13.2 4.2 copy-start.47
  17.3 205.1 %reduce-scatter.15.cloned.1.call-start = ((), (), s32[]{:S(2)}) async-start(), calls=%async_computation.11 | async-start | bytes 5898240 | tf_op jit(solution)/shard_map/reduce_scatter | solution.py:94
  21.7 137.6 %copy-start.30 = (pred[32,78]{1,0:T(8,128)(4,1)}, pred[32,78]{1,0:T(8,128)(4,1)S(1)}, u32[]{:S(2)}) copy-start(pred[32,78]{1,0:T(8,128)(4,1)S(1)} %iota_compare_fusion) | copy-start | bytes 7492
  146.7 3.7 copy-start.9
  146.7 11.9 %slice-start = ((s8[6291456]{0:T(1024)(128)(4,1)}), s8[4194304]{0:T(1024)(128)(4,1)S(1)}, s32[]{:S(2)}) async-start(s8[6291456]{0:T(1024)(128)(4,1)} %bitcast.86), calls=%async_computation.25 | async-start | bytes 8388608
  150.4 5.4 copy-start.11
  150.4 8.2 slice-start.1
  155.8 3.6 copy-start.5
  158.6 0.7 copy-start.18
  159.4 5.1 copy-start.15
  159.4 6.8 copy-start.22
  164.5 1.7 copy-start.16
  170.3 106.5 %all-gather.9.cloned.1.call-start = ((), (), s32[]{:S(2)}) async-start(), calls=%async_computation.14 | async-start | bytes 5750784 | tf_op jit(solution)/shard_map/all_gather | solution.py:112
  171.0 51.4 %copy-start.28 = (f32[768]{0:T(1024)S(1)}, f32[768]{0:T(1024)}, u32[]{:S(2)}) copy-start(f32[768]{0:T(1024)} %param.22) | copy-start | bytes 9220
  175.1 53.1 %copy-start.42 = (f32[768]{0:T(1024)S(1)}, f32[768]{0:T(1024)}, u32[]{:S(2)}) copy-start(f32[768]{0:T(1024)} %param.23) | copy-start | bytes 9220
  175.1 53.1 %copy-start.45 = (f32[768]{0:T(1024)S(1)}, f32[768]{0:T(1024)}, u32[]{:S(2)}) copy-start(f32[768]{0:T(1024)} %param.24) | copy-start | bytes 9220
  175.1 156.4 %all-gather.7.cloned.1.call-start = ((), (), s32[]{:S(2)}) async-start(), calls=%async_computation.12 | async-start | bytes 5750784 | tf_op jit(solution)/shard_map/all_gather | solution.py:100
  222.4 3.1 copy-start.2
  222.4 3.3 copy-start.6
  225.7 4.2 copy-start.24
  227.6 0.6 copy-start.32
  231.8 241.6 %reduce-scatter.19.cloned.1.call-start = ((), (), s32[]{:S(2)}) async-start(), calls=%async_computation.15 | async-start | bytes 5898240 | tf_op jit(solution)/shard_map/reduce_scatter | solution.py:120
  337.6 4.9 copy-start.48
  421.3 106.3 %reduce-scatter.17.cloned.1.call-start = ((), (), s32[]{:S(2)}) async-start(), calls=%async_computation.13 | async-start | bytes 5898240 | tf_op jit(solution)/shard_map/reduce_scatter | solution.py:106
  431.8 41.7 %copy-start.25 = (f32[16,78]{1,0:T(8,128)S(1)}, f32[16,78]{1,0:T(8,128)}, u32[]{:S(2)}) copy-start(f32[16,78]{1,0:T(8,128)} %copy-done.24) | copy-start | bytes 14980
  431.8 41.7 %copy-start.29 = (f32[768]{0:T(1024)S(1)}, f32[768]{0:T(1024)}, u32[]{:S(2)}) copy-start(f32[768]{0:T(1024)} %param.22) | copy-start | bytes 9220
  431.8 41.7 %copy-start.43 = (f32[768]{0:T(1024)S(1)}, f32[768]{0:T(1024)}, u32[]{:S(2)}) copy-start(f32[768]{0:T(1024)} %param.23) | copy-start | bytes 9220
  436.7 41.0 %copy-start.41 = (f32[16,78]{1,0:T(8,128)S(1)}, f32[16,78]{1,0:T(8,128)}, u32[]{:S(2)}) copy-start(f32[16,78]{1,0:T(8,128)} %copy-done.40) | copy-start | bytes 14980
  436.7 41.0 %copy-start.33 = (f32[16,78]{1,0:T(8,128)S(1)}, f32[16,78]{1,0:T(8,128)}, u32[]{:S(2)}) copy-start(f32[16,78]{1,0:T(8,128)} %copy-done.32) | copy-start | bytes 14980
  436.7 154.5 %all-gather.11.cloned.1.call-start = ((), (), s32[]{:S(2)}) async-start(), calls=%async_computation.16 | async-start | bytes 5750784 | tf_op jit(solution)/shard_map/all_gather | solution.py:126
  473.4 4.3 copy-start.3
  473.4 4.3 copy-start.7
  473.4 4.5 copy-start.14
  477.6 49.9 %copy-start.37 = (f32[16,78]{1,0:T(8,128)S(1)}, f32[16,78]{1,0:T(8,128)}, u32[]{:S(2)}) copy-start(f32[16,78]{1,0:T(8,128)} %copy-done.36) | copy-start | bytes 14980
  477.7 49.9 %copy-start.46 = (f32[768]{0:T(1024)S(1)}, f32[768]{0:T(1024)}, u32[]{:S(2)}) copy-start(f32[768]{0:T(1024)} %param.28) | copy-start | bytes 9220
  534.4 2.0 copy-start.8
  538.4 174.6 %reduce-scatter.27.cloned.1.call-start = ((), (), s32[]{:S(2)}) async-start(), calls=%async_computation.20 | async-start | bytes 2949120 | tf_op jit(solution)/shard_map/reduce_scatter | solution.py:192
  549.4 163.6 %reduce-scatter.29.cloned.1.call-start = ((), (), s32[]{:S(2)}) async-start(), calls=%async_computation.21 | async-start | bytes 2949120 | tf_op jit(solution)/shard_map/reduce_scatter | solution.py:198
  560.6 152.4 %reduce-scatter.25.cloned.1.call-start = ((), (), s32[]{:S(2)}) async-start(), calls=%async_computation.19 | async-start | bytes 737280 | tf_op jit(solution)/shard_map/reduce_scatter | solution.py:189
  597.3 5.1 copy-start.23
  615.0 6.9 copy-start.19
  615.0 6.9 copy-start.31
  632.2 5.5 copy-start.10
  637.7 2.9 copy-start.12
  640.6 5.2 copy-start.17
  640.6 5.2 copy-start.20
  656.4 82.7 %reduce-scatter.23.cloned.1.call-start = ((), (), s32[]{:S(2)}) async-start(), calls=%async_computation.18 | async-start | bytes 2211840 | tf_op jit(solution)/shard_map/reduce_scatter | solution.py:183
  709.3 63.2 %reduce-scatter.33.cloned.1.call-start = ((), (), s32[]{:S(2)}) async-start(), calls=%async_computation.23 | async-start | bytes 122880
  712.9 127.9 %all-reduce.5.cloned.1.call-start = ((), (), s32[]{:S(2)}) async-start(), calls=%async_computation.24 | async-start | bytes 3538944 | tf_op jit(solution)/shard_map/psum | solution.py:204
  739.1 154.9 %reduce-scatter.21.cloned.1.call-start = ((), (), s32[]{:S(2)}) async-start(), calls=%async_computation.17 | async-start | bytes 5898240 | tf_op jit(solution)/shard_map/reduce_scatter | solution.py:160
  760.9 0.7 copy-start.50
  760.9 169.3 %reduce-scatter.31.cloned.1.call-start = ((), (), s32[]{:S(2)}) async-start(), calls=%async_computation.22 | async-start | bytes 245760
  768.9 125.1 %copy-start.27 = (f32[16,78]{1,0:T(8,128)S(1)}, f32[16,78]{1,0:T(8,128)}, u32[]{:S(2)}) copy-start(f32[16,78]{1,0:T(8,128)} %copy-done.26) | copy-start | bytes 14980
  768.9 125.1 %copy-start.44 = (f32[768]{0:T(1024)S(1)}, f32[768]{0:T(1024)}, u32[]{:S(2)}) copy-start(f32[768]{0:T(1024)} %param.17) | copy-start | bytes 9220
  840.8 5.9 copy-start.21
  844.5 53.4 %copy-start.39 = (f32[16,78]{1,0:T(8,128)S(1)}, f32[16,78]{1,0:T(8,128)}, u32[]{:S(2)}) copy-start(f32[16,78]{1,0:T(8,128)} %copy-done.38) | copy-start | bytes 14980
  844.5 53.5 %copy-start.35 = (f32[16,78]{1,0:T(8,128)S(1)}, f32[16,78]{1,0:T(8,128)}, u32[]{:S(2)}) copy-start(f32[16,78]{1,0:T(8,128)} %copy-done.34) | copy-start | bytes 14980
  894.0 3.9 copy-start.4
  894.0 3.9 copy-start.13
  (4 other events, 2.4 us)
Sparse Core Ops, SparseCore 0:
  17.4 55.3 all-gather.4
  170.4 51.9 reduce-scatter.14
  224.1 52.6 all-gather.8
  278.8 52.6 all-gather.6
  421.4 51.9 reduce-scatter.18
  475.5 51.9 reduce-scatter.16
  538.5 52.6 all-gather.10
  593.9 33.0 reduce-scatter.26
  629.6 33.0 reduce-scatter.28
  665.7 22.0 reduce-scatter.24
  709.4 29.6 reduce-scatter.22
  741.9 19.5 reduce-scatter.32
  764.1 76.6 all-reduce.4
  843.0 50.9 reduce-scatter.20
  909.4 20.8 reduce-scatter.30
where the time goes:
time: 957 us; the launch traced here: 952 us
  waiting for transfers between devices  440 us (46%)
  local copies, waits for them, and re-layouts  212 us (22%)
  matrix products  183 us (19%)
  other arithmetic  74.3 us (8%)
  blocking collectives  25 us (3%)
  between operations  15.5 us (2%)
    psum x1, waiting for transfers between devices, local(): lax.psum(pieces[1].astype(jnp.bfloat16), 'outer').astype(jnp.float32)  67.5 us
    all_gather x1, waiting for transfers between devices, local(): gathered1 = lax.all_gather(normed1_low, 'tensor', axis=0, tiled=True)  51.2 us
    dot_general x4, matrix products, contract_cols(): lax.dot_general(left_side, right_side, (((1,), (1,)), ((), ())), preferre...  48.7 us
    reduce_scatter x1, waiting for transfers between devices, local(): lax.psum_scatter(attn_term.astype(jnp.bfloat16), 'tensor', scatter_dimens...  47.1 us
    reduce_scatter x1, waiting for transfers between devices, local(): lax.psum_scatter(norm1_term.astype(jnp.bfloat16), 'tensor', scatter_dimen...  46.2 us
    reduce_scatter x1, waiting for transfers between devices, local(): lax.psum_scatter(mlp_term.astype(jnp.bfloat16), 'tensor', scatter_dimensi...  46 us
    all_gather x1, waiting for transfers between devices, local(): mlp_rows = lax.all_gather(out_grad_low, 'tensor', axis=0, tiled=True)  44.9 us
    convert_element_type x3, local copies, waits for them, and re-layouts, local(): stacked.astype(jnp.bfloat16).reshape(token_count, 3 * head_width)  44.6 us
  transfers between devices with their start and end apart: 15, of which 11 were waited for; matrix products, arithmetic and copies ran while one was open for 26% of the time, Pallas kernels for 0%

commit v1 on v0

v1 whole, which is shorter than its diff:
```python
import functools

import jax
import jax.numpy as jnp
from jax import lax
from jax.experimental import pallas as pl
from jax.experimental.pallas import tpu as pltpu
from jax.sharding import PartitionSpec as P

F32 = jnp.float32
BF16 = jnp.bfloat16
HEAD_DIM = 64
SLOT = 80
QUAD = 4
BLOCKS = 3


def dot(left, right, dims):
    return lax.dot_general(left, right, (dims, ((), ())), preferred_element_type=F32)


NN = ((1,), (0,))
NT = ((1,), (1,))
TN = ((0,), (0,))


def rows_of(index, size):
    return pl.ds(pl.multiple_of(index * size, size), size)


def norm_stats(values):
    mean = jnp.mean(values, axis=-1, keepdims=True)
    centered = values - mean
    rstd = lax.rsqrt(jnp.mean(centered * centered, axis=-1, keepdims=True) + 1e-6)
    return centered * rstd, rstd


def norm_back(grad, values, gain):
    hat, rstd = norm_stats(values)
    scaled = grad * gain
    first = jnp.mean(scaled, axis=-1, keepdims=True)
    second = jnp.mean(scaled * hat, axis=-1, keepdims=True)
    back = rstd * (scaled - first - hat * second)
    gain_grad = jnp.sum(grad * hat, axis=0, keepdims=True)
    shift_grad = jnp.sum(grad, axis=0, keepdims=True)
    return back, gain_grad, shift_grad


def head_masks():
    head = lax.broadcasted_iota(jnp.int32, (SLOT, 256), 1) // HEAD_DIM
    return [[head == 0, head == 1, head == 2], [head == 1, head == 2, head == 3]]


def stack_heads(values, masks):
    zero = jnp.zeros_like(values)
    return jnp.concatenate([jnp.where(mask, values, zero) for mask in masks], axis=0)


def unstack_heads(values, masks):
    parts = [values[SLOT * i : SLOT * (i + 1)] for i in range(3)]
    return sum(jnp.where(mask, part, 0.0) for mask, part in zip(masks, parts))


def put_heads(ref, rows, start, first, second):
    ref[rows, start : start + 128] = first[:, :128].astype(BF16)
    ref[rows, start + 128 : start + 256] = (first[:, 128:] + second[:, :128]).astype(BF16)
    ref[rows, start + 256 : start + 384] = second[:, 128:].astype(BF16)


def attend(count_of, qkv, half, out, probs, scale, unroll):
    def one_image(image, carry):
        rows = rows_of(image, SLOT)
        live = lax.broadcasted_iota(jnp.int32, (SLOT, 3 * SLOT), 0) < count_of(image)
        parts = []
        for group, masks in enumerate(head_masks()):
            at = 128 * group
            query = qkv[half, rows, at : at + 256]
            key = qkv[half, rows, 384 + at : 384 + at + 256]
            value = qkv[half, rows, 768 + at : 768 + at + 256]
            scores = dot(key, stack_heads(query, masks), NT) * scale
            scores = jnp.where(live, scores, -1e9)
            top = jnp.max(scores, axis=0, keepdims=True)
            powers = jnp.exp(scores - top)
            weights = (powers / jnp.sum(powers, axis=0, keepdims=True)).astype(BF16)
            probs[rows_of((half * 16 + image) * 2 + group, SLOT), :] = weights
            parts.append(unstack_heads(dot(weights, value, TN), masks))
        put_heads(out, rows, half * 384, *parts)
        return carry

    lax.fori_loop(0, 16, one_image, 0, unroll=unroll)


def attend_back(qkv, half, out_grad, probs, scale, unroll):
    def one_image(image, carry):
        rows = rows_of(image, SLOT)
        queries, keys, values = [], [], []
        for group, masks in enumerate(head_masks()):
            at = 128 * group
            query = stack_heads(qkv[half, rows, at : at + 256], masks)
            key = qkv[half, rows, 384 + at : 384 + at + 256]
            value = qkv[half, rows, 768 + at : 768 + at + 256]
            grad = out_grad[rows, half * 384 + at : half * 384 + at + 256]
            grad = stack_heads(grad, masks)
            low = probs[rows_of((half * 16 + image) * 2 + group, SLOT), :]
            weights = low.astype(F32)
            prob_grad = dot(value, grad, NT)
            delta = jnp.sum(prob_grad * weights, axis=0, keepdims=True)
            score_grad = (weights * (prob_grad - delta)).astype(BF16)
            values.append(dot(low, grad, NN))
            keys.append(dot(score_grad, query, NN) * scale)
            queries.append(unstack_heads(dot(score_grad, key, TN), masks) * scale)
        put_heads(qkv.at[half], rows, 0, *queries)
        put_heads(qkv.at[half], rows, 384, *keys)
        put_heads(qkv.at[half], rows, 768, *values)
        return carry

    lax.fori_loop(0, 16, one_image, 0, unroll=unroll)


def layer_kernel(
    counts,
    tokens,
    cotangent,
    gain1,
    shift1,
    out_bias,
    gain2,
    shift2,
    down_bias,
    qkv_bias,
    up_bias,
    wqkv,
    wout,
    wup,
    wdown,
    mixed,
    tokens_grad,
    gqkv,
    gout,
    gup,
    gdown,
    vectors,
    qv_sum,
    up_sum,
    x_rows,
    gm,
    h1,
    qkv,
    att,
    probs,
    mid,
    h2,
    acc_y,
    acc_g,
    act,
    act_grad,
    stage_a,
    stage_b,
    mixed_part,
    grad_part,
    sems,
):
    width = x_rows.shape[1]
    tokens_all = x_rows.shape[0]
    quarter = tokens_all // QUAD
    images = tokens.shape[0]
    slots = tokens.shape[1]
    scale = HEAD_DIM**-0.5
    mine = lax.axis_index("tensor")

    def count_of(image):
        return counts[mine, image]

    pending = []

    def send(src, dst, index):
        copy = pltpu.make_async_copy(src, dst, sems.at[index])
        copy.start()
        pending.append(copy)

    def prepare(group, carry):
        for step in range(QUAD):
            image = group * QUAD + step
            base = pl.multiple_of(image * SLOT, SLOT)
            tail = pl.ds(pl.multiple_of(base + 64, 16), 16)
            x_rows[tail, :] = jnp.zeros((16, width), BF16)
            gm[tail, :] = jnp.zeros((16, width), BF16)
            x_rows[pl.ds(base, slots), :] = tokens[image]
            live = lax.broadcasted_iota(jnp.int32, (slots, width), 0) < count_of(image)
            gy = jnp.where(live, cotangent[image].astype(F32), 0.0)
            gm[pl.ds(base, slots), :] = gy.astype(BF16)
        return carry

    lax.fori_loop(0, images // QUAD, prepare, 0)
    vectors[...] = jnp.zeros_like(vectors)

    def first_norm(group, carry):
        rows = rows_of(group, quarter)
        hat, _ = norm_stats(x_rows[rows, :].astype(F32))
        h1[rows, :] = (hat * gain1[...] + shift1[...]).astype(BF16)
        vectors[5:6, :] += jnp.sum(gm[rows, :].astype(F32), axis=0, keepdims=True)
        return carry

    lax.fori_loop(0, QUAD, first_norm, 0)

    for half in range(2):
        for part in range(3):
            cols = slice(384 * part, 384 * (part + 1))
            found = dot(h1[...], wqkv[half, :, cols], NN)
            if part != 1:
                found = found + qkv_bias[half : half + 1, cols]
            qkv[half, :, cols] = found.astype(BF16)
        attend(count_of, qkv, half, att, probs, scale, 8)

    for part in range(2):
        cols = slice(384 * part, 384 * (part + 1))
        mid[:, cols] = (
            x_rows[:, cols].astype(F32) + dot(att[...], wout[:, cols], NN) + out_bias[:, cols]
        )

    def second_norm(group, carry):
        rows = rows_of(group, quarter)
        hat, _ = norm_stats(mid[rows, :])
        h2[rows, :] = (hat * gain2[...] + shift2[...]).astype(BF16)
        return carry

    lax.fori_loop(0, QUAD, second_norm, 0)

    for half in range(2):
        for block in range(BLOCKS):
            index = half * BLOCKS + block
            bias = up_bias[index : index + 1, :]

            def hidden(group, total, index=index, bias=bias):
                rows = rows_of(group, quarter)
                u = dot(h2[rows, :], wup[index], NN) + bias
                cdf = 0.5 * (1.0 + lax.erf(u * 0.7071067811865476))
                act[rows, :] = (u * cdf).astype(BF16)
                slope = cdf + u * jnp.exp(-0.5 * u * u) * 0.3989422804014327
                low = (dot(gm[rows, :], wdown[index], NT) * slope).astype(BF16)
                act_grad[rows, :] = low
                return total + jnp.sum(low.astype(F32), axis=0, keepdims=True)

            total = lax.fori_loop(0, QUAD, hidden, jnp.zeros((1, 512), F32))
            up_sum[index : index + 1, :] = total
            for part in range(2):
                cols = slice(384 * part, 384 * (part + 1))
                y = dot(act[...], wdown[index, :, cols], NN)
                g = dot(act_grad[...], wup[index, cols, :], NT)
                if index == 0:
                    acc_y[:, cols] = y
                    acc_g[:, cols] = g
                else:
                    acc_y[:, cols] += y
                    acc_g[:, cols] += g
            slot = index % 2
            if index >= 2:
                pending.pop(0).wait()
                pending.pop(0).wait()
            stage_a[slot, 0, :, :512] = dot(h2[...], act_grad[...], TN).astype(BF16)
            send(stage_a.at[slot, 0, :, pl.ds(0, 512)], gup.at[index], 2 * slot)
            stage_a[slot, 1, :, :512] = dot(gm[...], act[...], TN).astype(BF16)
            send(stage_a.at[slot, 1, :, pl.ds(0, 512)], gdown.at[index], 2 * slot + 1)

    def ship(part, whole, group, index):
        slot = lax.rem(group, 2)
        return pltpu.make_async_copy(
            part.at[slot], whole.at[pl.ds(group * QUAD, QUAD)], sems.at[index + slot]
        )

    def before(part, whole, group, index):
        @pl.when(group >= 2)
        def _():
            ship(part, whole, group - 2, index).wait()

    def after(part, whole, index):
        for group in (QUAD - 2, QUAD - 1):
            ship(part, whole, jnp.int32(group), index).wait()

    def finish(group, carry):
        rows = rows_of(group, quarter)
        before(mixed_part, mixed, group, 6)
        values = mid[rows, :]
        y = (values + acc_y[rows, :] + down_bias[...]).astype(BF16)
        for step in range(QUAD):
            mixed_part[lax.rem(group, 2), step] = y[SLOT * step : SLOT * step + slots]
        ship(mixed_part, mixed, group, 6).start()
        back, gain_grad, shift_grad = norm_back(acc_g[rows, :], values, gain2[...])
        grad = gm[rows, :].astype(F32) + back
        acc_g[rows, :] = grad
        gm[rows, :] = grad.astype(BF16)
        vectors[2:3, :] += jnp.sum(grad, axis=0, keepdims=True)
        vectors[3:4, :] += gain_grad
        vectors[4:5, :] += shift_grad
        return carry

    lax.fori_loop(0, QUAD, finish, 0)
    after(mixed_part, mixed, 6)

    out_grad = h2
    for part in range(2):
        cols = slice(384 * part, 384 * (part + 1))
        out_grad[:, cols] = dot(gm[...], wout[cols, :], NT).astype(BF16)
    while pending:
        pending.pop(0).wait()
    stage_a[0, 0] = dot(att[...], gm[...], TN).astype(BF16)
    send(stage_a.at[0, 0], gout, 0)

    for half in range(2):
        attend_back(qkv, half, out_grad, probs, scale, 8)
        for part in range(3):
            cols = slice(384 * part, 384 * (part + 1))
            grads = qkv[half, :, cols]
            stage_b[half, :, cols] = dot(h1[...], grads, TN).astype(BF16)
            if part != 1:
                at = part // 2
                qv_sum[2 * half + at : 2 * half + at + 1, :] = jnp.sum(
                    grads.astype(F32), axis=0, keepdims=True
                )
        send(stage_b.at[half], gqkv.at[half], 4 + half)

    for part in range(2):
        cols = slice(384 * part, 384 * (part + 1))
        acc_y[:, cols] = dot(qkv[0], wqkv[0, cols, :], NT)
        acc_y[:, cols] += dot(qkv[1], wqkv[1, cols, :], NT)

    def last_norm(group, carry):
        rows = rows_of(group, quarter)
        before(grad_part, tokens_grad, group, 8)
        values = x_rows[rows, :].astype(F32)
        back, gain_grad, shift_grad = norm_back(acc_y[rows, :], values, gain1[...])
        grad = acc_g[rows, :] + back
        for step in range(QUAD):
            grad_part[lax.rem(group, 2), step] = grad[SLOT * step : SLOT * step + slots]
        ship(grad_part, tokens_grad, group, 8).start()
        vectors[0:1, :] += gain_grad
        vectors[1:2, :] += shift_grad
        return carry

    lax.fori_loop(0, QUAD, last_norm, 0)
    after(grad_part, tokens_grad, 8)
    while pending:
        pending.pop(0).wait()


def run_layer(counts, tokens, cotangent, rows, qkv_bias, up_bias, wqkv, wout, wup, wdown):
    images, slots, width = tokens.shape
    total = images * SLOT
    half = wqkv.shape[2]
    vmem = pl.BlockSpec(memory_space=pltpu.VMEM)
    anywhere = pl.BlockSpec(memory_space=pl.ANY)
    shape = jax.ShapeDtypeStruct
    return pl.pallas_call(
        layer_kernel,
        out_shape=[
            shape((images, slots, width), BF16),
            shape((images, slots, width), F32),
            shape(wqkv.shape, BF16),
            shape(wout.shape, BF16),
            shape(wup.shape, BF16),
            shape(wup.shape, BF16),
            shape((8, width), F32),
            shape((4, half // 3), F32),
            shape(up_bias.shape, F32),
        ],
        in_specs=[pl.BlockSpec(memory_space=pltpu.SMEM)] + [vmem] * 14,
        out_specs=[anywhere] * 6 + [vmem] * 3,
        scratch_shapes=[
            pltpu.VMEM((total, width), BF16),
            pltpu.VMEM((total, width), BF16),
            pltpu.VMEM((total, width), BF16),
            pltpu.VMEM((2, total, half), BF16),
            pltpu.VMEM((total, width), BF16),
            pltpu.VMEM((4 * images * SLOT, 3 * SLOT), BF16),
            pltpu.VMEM((total, width), F32),
            pltpu.VMEM((total, width), BF16),
            pltpu.VMEM((total, width), F32),
            pltpu.VMEM((total, width), F32),
            pltpu.VMEM((total, 512), BF16),
            pltpu.VMEM((total, 512), BF16),
            pltpu.VMEM((2, 2, width, width), BF16),
            pltpu.VMEM((2, width, half), BF16),
            pltpu.VMEM((2, QUAD, slots, width), BF16),
            pltpu.VMEM((2, QUAD, slots, width), F32),
            pltpu.SemaphoreType.DMA((10,)),
        ],
        compiler_params=pltpu.CompilerParams(vmem_limit_bytes=64 * 2**20 - 2**17),
    )(counts, tokens, cotangent, *rows, qkv_bias, up_bias, wqkv, wout, wup, wdown)


def local(
    tokens,
    counts,
    norm1_gain,
    norm1_shift,
    qkv_weight,
    qv_bias,
    out_weight,
    out_bias,
    norm2_gain,
    norm2_shift,
    up_weight,
    up_bias,
    down_weight,
    down_bias,
    cotangent,
):
    width = tokens.shape[2]
    inner = lax.axis_size("inner")
    head_width = qkv_weight.shape[2]
    hidden = up_weight.shape[1]

    def both(own):
        other = lax.ppermute(own, "tensor", [(0, 1), (1, 0)])
        return jnp.stack([own, other])

    wqkv = both(qkv_weight.reshape(width, 3 * head_width))
    wout = both(out_weight).reshape(2 * head_width, width)
    cut = (4, BLOCKS, 128)
    wup = both(
        up_weight.reshape(width, *cut).transpose(2, 0, 1, 3).reshape(BLOCKS, width, 512)
    ).reshape(2 * BLOCKS, width, 512)
    wdown = both(
        down_weight.reshape(*cut, width).transpose(1, 0, 2, 3).reshape(BLOCKS, 512, width)
    ).reshape(2 * BLOCKS, 512, width)
    up_rows = both(up_bias.reshape(cut).transpose(1, 0, 2).reshape(BLOCKS, 512)).reshape(
        2 * BLOCKS, 512
    )
    zero = jnp.zeros_like(qv_bias[0])
    qkv_rows = both(jnp.concatenate([qv_bias[0], zero, qv_bias[1]]))
    rows = [
        v.reshape(1, width)
        for v in (norm1_gain, norm1_shift, out_bias, norm2_gain, norm2_shift, down_bias)
    ]
    mixed, tokens_grad, gqkv, gout, gup, gdown, vectors, qv_sum, up_sum = run_layer(
        counts, tokens, cotangent, rows, qkv_rows, up_rows, wqkv, wout, wup, wdown
    )

    def own_half(grads):
        other = lax.ppermute(grads[1].astype(BF16), "tensor", [(0, 1), (1, 0)])
        return (grads[0].astype(F32) + other.astype(F32)).astype(BF16)

    gqkv = own_half(gqkv)
    gout = own_half(gout.reshape(2, head_width, width))
    back = lambda v: v.reshape(BLOCKS, width, 4, 128).transpose(1, 2, 0, 3).reshape(width, hidden)
    gup = back(own_half(gup.reshape(2, BLOCKS, width, 512)))
    gdown = back(own_half(gdown.reshape(2, BLOCKS, width, 512))).T
    qv_sum = own_half(qv_sum.reshape(2, 2, head_width))
    up_sum = own_half(up_sum.reshape(2, BLOCKS, 512))
    up_sum = up_sum.reshape(BLOCKS, 4, 128).transpose(1, 0, 2).reshape(hidden)
    vectors = lax.psum(vectors.astype(BF16), "tensor")

    def reduce(grads, dim=0):
        part = lax.psum_scatter(grads, "inner", scatter_dimension=dim, tiled=True)
        return lax.psum(part, "outer").astype(F32)

    gqkv = reduce(gqkv).reshape(width // inner, 3, head_width)
    gout = reduce(gout)
    gup = reduce(gup)
    gdown = reduce(gdown)
    vectors = reduce(vectors.T)
    qv_sum = reduce(qv_sum.T).T
    up_sum = reduce(up_sum)
    return (
        mixed,
        tokens_grad,
        vectors[:, 0],
        vectors[:, 1],
        gqkv,
        qv_sum,
        gout,
        vectors[:, 2],
        vectors[:, 3],
        vectors[:, 4],
        gup,
        up_sum,
        gdown,
        vectors[:, 5],
    )


def solution(mesh):
    in_specs = (
        P(("tensor", "inner", "outer"), None, None),
        P(None, ("inner", "outer")),
        P(),
        P(),
        P(None, None, "tensor"),
        P(None, "tensor"),
        P("tensor", None),
        P(),
        P(),
        P(),
        P(None, "tensor"),
        P("tensor"),
        P("tensor", None),
        P(),
        P(("tensor", "inner", "outer"), None, None),
    )
    out_specs = (
        P(("tensor", "inner", "outer"), None, None),
        P(("tensor", "inner", "outer"), None, None),
        P("inner"),
        P("inner"),
        P("inner", None, "tensor"),
        P(None, ("tensor", "inner")),
        P(("tensor", "inner"), None),
        P("inner"),
        P("inner"),
        P("inner"),
        P("inner", "tensor"),
        P(("tensor", "inner")),
        P(("tensor", "inner"), None),
        P("inner"),
    )
    return jax.shard_map(local, mesh=mesh, in_specs=in_specs, out_specs=out_specs, check_vma=False)
```

time: 957 us -> 704 us (0.74)
  matrix products: 183 us -> 0 us
  local copies, waits for them, and re-layouts: 212 us -> 74.8 us
  Pallas kernels: 0 us -> 123 us
  other arithmetic: 74.3 us -> 27 us
  waiting for transfers between devices: 440 us -> 416 us
  starting transfers between devices: 1.43 us -> 16.8 us
    ppermute x0 -> x12, waiting for transfers between devices: none -> 279 us  [the longest x6 149 us: own_half(): other = lax.ppermute(grads[1].astype(BF16), 'tensor', [(0, 1), (1, 0)])]
    dot_general x18 -> x0, matrix products: 183 us -> none  [the longest x4 48.7 us: contract_cols(): lax.dot_general(left_side, right_side, (((1,), (1,)), ((), ())), preferre...]
    reduce_scatter x8 -> x3, waiting for transfers between devices: 202 us -> 36.7 us  [reduce(): part = lax.psum_scatter(grads, 'inner', scatter_dimension=dim, tiled=True)]
    all_gather x4 -> x0, waiting for transfers between devices: 158 us -> none  [the longest x1 51.2 us: local(): gathered1 = lax.all_gather(normed1_low, 'tensor', axis=0, tiled=True)]
    pallas_call x0 -> x1, Pallas kernels: none -> 123 us  [run_layer(): pl.pallas_call(layer_kernel, out_shape=[shape((images, slots, width), BF1...]
    convert_element_type x13 -> x0, local copies, waits for them, and re-layouts: 87.7 us -> none  [the longest x3 44.6 us: local(): stacked.astype(jnp.bfloat16).reshape(token_count, 3 * head_width)]
    reduce_sum x11 -> x0, other arithmetic: 36.3 us -> none  [the longest x4 14.9 us: layer_norm(): return centered * lax.rsqrt(variance + 1e-06) * norm_gain + norm_shift]
    all_gather x4 -> x0, local copies, waits for them, and re-layouts: 24.3 us -> none  [the longest x1 6.07 us: local(): mlp_rows = lax.all_gather(out_grad_low, 'tensor', axis=0, tiled=True)]
  transfers between devices with their start and end apart: 15 -> 19, of which waited for: 11 -> 11; matrix products, arithmetic and copies ran while one was open for 26% -> 12% of each run, Pallas kernels for 0% -> 0%
where the time goes in v1:
time: 704 us; the launch traced here: 696 us
  waiting for transfers between devices  416 us (59%)
  Pallas kernels  123 us (17%)
  local copies, waits for them, and re-layouts  74.8 us (11%)
  other arithmetic  27 us (4%)
  blocking collectives  23.3 us (3%)
  starting transfers between devices  16.8 us (2%)
  between operations  15.3 us (2%)
    ppermute x6, waiting for transfers between devices, own_half(): other = lax.ppermute(grads[1].astype(BF16), 'tensor', [(0, 1), (1, 0)])  149 us
    ppermute x6, waiting for transfers between devices, both(): other = lax.ppermute(own, 'tensor', [(0, 1), (1, 0)])  130 us
    pallas_call x1, Pallas kernels, run_layer(): pl.pallas_call(layer_kernel, out_shape=[shape((images, slots, width), BF1...  123 us
    psum x1, waiting for transfers between devices, reduce(): return lax.psum(part, 'outer').astype(F32)  73 us
    reduce_scatter x3, waiting for transfers between devices, reduce(): part = lax.psum_scatter(grads, 'inner', scatter_dimension=dim, tiled=True)  36.7 us
    unnamed x52, local copies, waits for them, and re-layouts  31.8 us
    unnamed x10, waiting for transfers between devices  26.9 us
    another operation x6, other arithmetic, both(): return jnp.stack([own, other])  16.6 us
  transfers between devices with their start and end apart: 19, of which 11 were waited for; matrix products, arithmetic and copies ran while one was open for 12% of the time, Pallas kernels for 0%

profile of v1, /device:TPU:0, one launch (start us, length us, event | category | flops | bytes accessed | tf_op | source)
XLA Modules:
  0.0 695.8 jit_solution(10149722521378384777)
XLA Ops:
  7.2 2.8 copy.81
  10.1 1.6 copy.82
  11.7 3.0 collective-permute-start.4
  14.7 2.6 copy.77
  17.3 2.2 copy.79
  19.5 3.2 copy.85
  22.7 2.0 collective-permute-start.5
  24.8 2.1 collective-permute-start
  26.9 1.0 copy.80
  27.9 0.7 reshape.136
  28.7 3.6 copy.87.tokens
  32.3 1.9 copy.88.cotangent
  37.7 129.8 %collective-permute-done = f32[1152]{0:T(1024)} collective-permute-done((f32[1152]{0:T(1024)S(1)}, f32[1152]{0:T(1024)}, u32[]{:S(2)}, u32[]{:S(2)}) %collective-permute-start) | collective-permute-done | bytes 4640 | tf_op jit(solution)/shard_map/ppermute | solution.py:414
  167.5 1.7 collective-permute-start.1
  169.3 0.7 stack.43
  171.2 0.6 reshape.138.up_bias
  171.8 2.4 pad_maximum_fusion.3
  174.2 3.6 pad_maximum_fusion.2.wqkv
  177.8 4.9 pad_maximum_fusion
  182.7 6.7 copy.84
  189.4 5.0 pad_maximum_fusion.1
  194.5 122.8 %shard_map.254 = (bf16[16,78,768]{2,1,0:T(8,128)(2,1)}, f32[16,78,768]{2,1,0:T(8,128)}, bf16[2,768,1152]{2,1,0:T(8,128)(2,1)}, bf16[768,768]{1,0:T(8,128)(2,1)},...) custom-call(s32[2,16]{1,0:T(2,128)} %counts.1, ...), custom_call_target="tpu_custom_call" | custom-call | tf_op jit(solution)/shard_map/pallas_call | solution.py:353
  317.3 1.8 slice_bitcast_fusion
  319.1 1.8 collective-permute-start.6
  320.9 36.9 %collective-permute-done.6 = bf16[768,1152]{1,0:T(8,128)(2,1)S(1)} collective-permute-done((bf16[768,1152]{1,0:T(8,128)(2,1)S(1)}, bf16[768,1152]{1,0:T(8,128)(2,1)S(1)}, u32[]{:S(2)}, u32[]{:S(2)}) %collective-permute-start.6) | collective-permute-done | bytes 1769504 | tf_op jit(solution)/shard_map/ppermute | solution.py:440
  357.8 1.7 fusion
  359.5 2.0 slice.86
  361.5 1.5 collective-permute-start.9
  363.0 48.9 %collective-permute-done.9 = bf16[3,768,512]{2,1,0:T(8,128)(2,1)S(1)} collective-permute-done((bf16[3,768,512]{2,1,0:T(8,128)(2,1)S(1)}, bf16[3,768,512]{2,1,0:T(8,128)(2,1)S(1)}, u32[]{:S(2)}, u32[]{:S(2)}) %collective-permute-start.9) | collective-permute-done | bytes 2359328 | tf_op jit(solution)/shard_map/ppermute | solution.py:440
  412.0 0.7 add_convert_fusion.1
  412.6 2.1 reshape.149
  414.8 4.1 copy.89
  418.9 2.4 copy.98
  421.4 1.9 slice.90
  423.3 1.2 collective-permute-start.11
  424.5 1.0 collective-permute-start.8
  425.5 59.9 %collective-permute-done.8 = bf16[384,768]{1,0:T(8,128)(2,1)S(1)} collective-permute-done((bf16[384,768]{1,0:T(8,128)(2,1)S(1)}, bf16[384,768]{1,0:T(8,128)(2,1)S(1)}, u32[]{:S(2)}, u32[]{:S(2)}) %collective-permute-start.8) | collective-permute-done | bytes 589856 | tf_op jit(solution)/shard_map/ppermute | solution.py:440
  485.5 1.0 add_convert_fusion.2
  486.5 3.0 add_convert_fusion
  489.6 2.4 reshape.153
  492.0 5.6 copy.91
  498.2 0.7 collective-permute-start.7
  499.0 2.8 collective-permute-done.7
  501.8 0.8 copy.96
  502.7 0.8 copy.100
  503.6 2.1 reshape.147
  505.7 2.2 copy.99
  508.0 1.2 reduce-scatter.15.cloned.1.call-done
  509.2 35.5 %reduce-scatter.17.cloned.1.call-done = bf16[384,768]{1,0:T(8,128)(2,1)} async-done(((bf16[1536,768]{1,0:T(8,128)(2,1)}), bf16[384,768]{1,0:T(8,128)(2,1)}) %reduce-scatter.17.cloned.1.call-update) | async-done | bytes 589840 | tf_op jit(solution)/shard_map/reduce_scatter | solution.py:454
  544.7 1.5 collective-permute-start.10
  547.5 6.4 copy.93
  553.9 1.8 copy.92
  555.8 6.0 all-reduce
  561.8 4.8 reduce-scatter.19.cloned.1.call-done
  566.6 0.8 copy.97
  567.5 22.0 %reduce-scatter.23.cloned.1.call-done = bf16[192,8]{1,0:T(8,128)(2,1)} async-done(((bf16[768,8]{1,0:T(8,128)(2,1)}), bf16[192,8]{1,0:T(8,128)(2,1)}) %reduce-scatter.23.cloned.1.call-update) | async-done | bytes 3088
  589.4 0.8 copy.101
  590.3 4.9 psum.64
  595.2 12.4 %all-reduce.1 = (bf16[192,8]{0,1:T(8,128)(2,1)S(1)}, bf16[2,96]{1,0:T(2,128)(2,1)S(1)}, bf16[384]{0:T(512)(128)(2,1)S(1)}) all-reduce(bf16[192,8]{0,1:T(8,128)(2,1)S(1)} %psum.64, bf16[2,96]{1,0:T(2,128)(2,1)S(1)} %bitcast.70, bf16[384]{0:T(512)(128)(2,1)S(1)} %dynamic-slice.1), channel_id=1, replica_groups=mesh['tensor'=2,'inner'=4,'outer'=4] {'outer'}, use_global_device_ids=true, to_apply=%region_2.0 | all-reduce | flops 2112 | bytes 8448 | tf_op jit(solution)/shard_map/psum | solution.py:455
  609.4 73.0 %all-reduce.5.cloned.1.call-done = (bf16[192,3,384]{2,1,0:T(4,128)(2,1)}, bf16[192,1536]{0,1:T(8,128)(2,1)}, bf16[96,768]{1,0:T(8,128)(2,1)}, bf16[384,768]{1,0:T(8,128)(2,1)}) async-done(((bf16[192,3,384]{2,1,0:T(4,128)(2,1)}, bf16[192,1536]{0,1:T(8,128)(2,1)}, bf16[96,768]{1,0:T(8,128)(2,1)}, bf16[384,768]{1,0:T(8,128)(2,1)}), (bf16[192,3,384]{2,1,0:T(4,128)(2,1)}, bf16[192,1536]{0,1:T(8,128)(2,1)}, ...) | async-done | bytes 1769488 | tf_op jit(solution)/shard_map/psum | solution.py:455
  682.4 2.2 convert_element_type.95
  684.6 2.4 copy.95
  687.0 1.0 copy.94
  688.0 0.7 convert_element_type.84
  (85 shorter events, 8.4 us)
Async XLA Ops:
  7.2 496.4 %reduce-scatter.13.cloned.1.call-start = ((), (), s32[]{:S(2)}) async-start(), calls=%async_computation.6 | async-start | bytes 2211840 | tf_op jit(solution)/shard_map/reduce_scatter | solution.py:454
  11.7 166.1 %collective-permute-start.4 = (bf16[3,768,512]{1,2,0:T(8,128)(2,1)}, bf16[3,768,512]{1,2,0:T(8,128)(2,1)}, u32[]{:S(2)}, u32[]{:S(2)}) collective-permute-start(bf16[3,768,512]{1,2,0:T(8,128)(2,1)} %bitcast.16), channel_id=1, source_target_pairs={{0,16},{16,0},{1,17},{17,1},{2,18},{18,2},{3,19},{19,3},{4,20},{20... | collective-permute-start | bytes 7077896 | tf_op jit(solution)/shard_map/ppermute | solution.py:414
  19.5 154.7 %collective-permute-start.2 = (bf16[768,1152]{1,0:T(8,128)(2,1)}, bf16[768,1152]{1,0:T(8,128)(2,1)}, u32[]{:S(2)}, u32[]{:S(2)}) collective-permute-start(bf16[768,1152]{1,0:T(8,128)(2,1)} %copy.79), channel_id=1, source_target_pairs={{0,16},{16,0},{1,17},{17,1},{2,18},{18,2},{3,19},{19,3},{4,20},{20... | collective-permute-start | bytes 5308424 | tf_op jit(solution)/shard_map/ppermute | solution.py:414
  19.5 5.3 copy-start.16
  22.7 166.7 %collective-permute-start.5 = (bf16[3,512,768]{2,1,0:T(8,128)(2,1)}, bf16[3,512,768]{2,1,0:T(8,128)(2,1)}, u32[]{:S(2)}, u32[]{:S(2)}) collective-permute-start(bf16[3,512,768]{2,1,0:T(8,128)(2,1)} %bitcast.22), channel_id=1, source_target_pairs={{0,16},{16,0},{1,17},{17,1},{2,18},{18,2},{3,19},{19,3},{4,20},{20... | collective-permute-start | bytes 7077896 | tf_op jit(solution)/shard_map/ppermute | solution.py:414
  24.8 147.0 %collective-permute-start.3 = (bf16[384,768]{1,0:T(8,128)(2,1)}, bf16[384,768]{1,0:T(8,128)(2,1)}, u32[]{:S(2)}, u32[]{:S(2)}) collective-permute-start(bf16[384,768]{1,0:T(8,128)(2,1)} %param.21), channel_id=1, source_target_pairs={{0,16},{16,0},{1,17},{17,1},{2,18},{18,2},{3,19},{19,3},{4,20},{20... | collective-permute-start | bytes 1769480 | tf_op jit(solution)/shard_map/ppermute | solution.py:414
  24.8 142.7 %collective-permute-start = (f32[1152]{0:T(1024)S(1)}, f32[1152]{0:T(1024)}, u32[]{:S(2)}, u32[]{:S(2)}) collective-permute-start(f32[1152]{0:T(1024)S(1)} %pad_maximum_fusion.6), channel_id=1, source_target_pairs={{0,16},{16,0},{1,17},{17,1},{2,18},{18,2},{3,19},{19,3},{4,20},{20... | collective-permute-start | bytes 13832 | tf_op jit(solution)/shard_map/ppermute | solution.py:414
  28.7 3.6 copy-start.3
  32.3 1.9 copy-start.9
  32.3 2.5 copy-start.10
  32.3 3.1 copy-start.11
  32.3 3.7 copy-start.12
  32.3 4.3 copy-start.13
  32.3 4.8 copy-start.14
  167.5 3.7 collective-permute-start.1
  317.3 40.5 %copy-start.1 = (bf16[2,768,1152]{2,1,0:T(8,128)(2,1)S(1)}, bf16[2,768,1152]{2,1,0:T(8,128)(2,1)}, u32[]{:S(2)}) copy-start(bf16[2,768,1152]{2,1,0:T(8,128)(2,1)} %get-tuple-element.26) | copy-start | bytes 10616836
  319.1 38.7 %collective-permute-start.6 = (bf16[768,1152]{1,0:T(8,128)(2,1)S(1)}, bf16[768,1152]{1,0:T(8,128)(2,1)S(1)}, u32[]{:S(2)}, u32[]{:S(2)}) collective-permute-start(bf16[768,1152]{1,0:T(8,128)(2,1)S(1)} %slice_bitcast_fusion), channel_id=1, source_target_pairs={{0,16},{16,0},{1,17},{17,1},{2,18},{18,2},{3,19},{19,3},{4,20},{20... | collective-permute-start | bytes 5308424 | tf_op jit(solution)/shard_map/ppermute | solution.py:440
  359.5 146.3 %reduce-scatter.21.cloned.1.call-start = ((), (), s32[]{:S(2)}) async-start(), calls=%async_computation.10 | async-start | bytes 2949120
  359.5 52.4 %copy-start = (bf16[6,768,512]{2,1,0:T(8,128)(2,1)S(1)}, bf16[6,768,512]{2,1,0:T(8,128)(2,1)}, u32[]{:S(2)}) copy-start(bf16[6,768,512]{2,1,0:T(8,128)(2,1)} %get-tuple-element.29) | copy-start | bytes 14155780
  361.5 50.4 %collective-permute-start.9 = (bf16[3,768,512]{2,1,0:T(8,128)(2,1)S(1)}, bf16[3,768,512]{2,1,0:T(8,128)(2,1)S(1)}, u32[]{:S(2)}, u32[]{:S(2)}) collective-permute-start(bf16[3,768,512]{2,1,0:T(8,128)(2,1)S(1)} %slice.86), channel_id=1, source_target_pairs={{0,16},{16,0},{1,17},{17,1},{2,18},{18,2},{3,19},{19,3},{4,20},{20... | collective-permute-start | bytes 7077896 | tf_op jit(solution)/shard_map/ppermute | solution.py:440
  421.3 87.9 %reduce-scatter.15.cloned.1.call-start = ((), (), s32[]{:S(2)}) async-start(), calls=%async_computation.7 | async-start | bytes 737280 | tf_op jit(solution)/shard_map/reduce_scatter | solution.py:454
  421.4 3.1 copy-start.4
  423.3 63.2 %collective-permute-start.11 = (bf16[3,768,512]{2,1,0:T(8,128)(2,1)S(1)}, bf16[3,768,512]{2,1,0:T(8,128)(2,1)}, u32[]{:S(2)}, u32[]{:S(2)}) collective-permute-start(bf16[3,768,512]{2,1,0:T(8,128)(2,1)S(1)} %slice.90), channel_id=1, source_target_pairs={{0,16},{16,0},{1,17},{17,1},{2,18},{18,2},{3,19},{19,3},{4,20},{20... | collective-permute-start | bytes 7077896 | tf_op jit(solution)/shard_map/ppermute | solution.py:440
  424.5 60.9 %collective-permute-start.8 = (bf16[384,768]{1,0:T(8,128)(2,1)S(1)}, bf16[384,768]{1,0:T(8,128)(2,1)S(1)}, u32[]{:S(2)}, u32[]{:S(2)}) collective-permute-start(bf16[384,768]{1,0:T(8,128)(2,1)S(1)} %slice.81), channel_id=1, source_target_pairs={{0,16},{16,0},{1,17},{17,1},{2,18},{18,2},{3,19},{19,3},{4,20},{20... | collective-permute-start | bytes 1769480 | tf_op jit(solution)/shard_map/ppermute | solution.py:440
  486.5 58.2 %reduce-scatter.17.cloned.1.call-start = ((), (), s32[]{:S(2)}) async-start(), calls=%async_computation.8 | async-start | bytes 2949120 | tf_op jit(solution)/shard_map/reduce_scatter | solution.py:454
  497.5 0.7 copy-start.15
  497.5 5.2 copy-start.7
  497.6 69.1 %reduce-scatter.19.cloned.1.call-start = ((), (), s32[]{:S(2)}) async-start(), calls=%async_computation.9 | async-start | bytes 122880
  498.2 3.6 collective-permute-start.7
  502.6 86.8 %reduce-scatter.23.cloned.1.call-start = ((), (), s32[]{:S(2)}) async-start(), calls=%async_computation.11 | async-start | bytes 245760
  503.5 41.2 %copy-start.8 = (f32[6,512]{1,0:T(8,128)S(1)}, f32[6,512]{1,0:T(8,128)}, u32[]{:S(2)}) copy-start(f32[6,512]{1,0:T(8,128)} %get-tuple-element.30) | copy-start | bytes 36868
  503.5 42.7 %copy-start.17 = (u32[32]{0:T(128)S(1)}, u32[32]{0:T(128)}, u32[]{:S(2)}) copy-start(u32[32]{0:T(128)} %constant.6) | copy-start | bytes 388
  503.5 178.9 %all-reduce.5.cloned.1.call-start = ((), (), s32[]{:S(2)}) async-start(), calls=%async_computation.12 | async-start | bytes 4227072 | tf_op jit(solution)/shard_map/psum | solution.py:455
  544.7 11.0 %collective-permute-start.10 = (bf16[3,512]{1,0:T(4,128)(2,1)S(1)}, bf16[3,512]{1,0:T(4,128)(2,1)S(1)}, u32[]{:S(2)}, u32[]{:S(2)}) collective-permute-start(bf16[3,512]{1,0:T(4,128)(2,1)S(1)} %slice.115), channel_id=1, source_target_pairs={{0,16},{16,0},{1,17},{17,1},{2,18},{18,2},{3,19},{19,3},{4,20},{20... | collective-permute-start | bytes 9224 | tf_op jit(solution)/shard_map/ppermute | solution.py:440
  547.5 6.4 copy-start.2
  682.4 4.6 copy-start.5
  682.4 5.6 copy-start.6
Sparse Core Ops, SparseCore 0:
  359.6 30.5 reduce-scatter.12
  421.5 33.8 reduce-scatter.20
  486.6 22.5 reduce-scatter.14
  511.6 33.0 reduce-scatter.16
  547.1 19.5 reduce-scatter.18
  569.7 19.7 reduce-scatter.22
  593.4 88.9 all-reduce.4

commit v2 on v1

v2 whole, which is shorter than its diff:
```python
import functools

import jax
import jax.numpy as jnp
from jax import lax
from jax.experimental import pallas as pl
from jax.experimental.pallas import tpu as pltpu
from jax.sharding import PartitionSpec as P

F32 = jnp.float32
BF16 = jnp.bfloat16
HEAD_DIM = 64
SLOT = 80
QUAD = 4
MESH = pl.DeviceIdType.MESH
BLOCKS = 3


def dot(left, right, dims):
    return lax.dot_general(left, right, (dims, ((), ())), preferred_element_type=F32)


NN = ((1,), (0,))
NT = ((1,), (1,))
TN = ((0,), (0,))


def rows_of(index, size):
    return pl.ds(pl.multiple_of(index * size, size), size)


def norm_stats(values):
    mean = jnp.mean(values, axis=-1, keepdims=True)
    centered = values - mean
    rstd = lax.rsqrt(jnp.mean(centered * centered, axis=-1, keepdims=True) + 1e-6)
    return centered * rstd, rstd


def norm_back(grad, values, gain):
    hat, rstd = norm_stats(values)
    scaled = grad * gain
    first = jnp.mean(scaled, axis=-1, keepdims=True)
    second = jnp.mean(scaled * hat, axis=-1, keepdims=True)
    back = rstd * (scaled - first - hat * second)
    gain_grad = jnp.sum(grad * hat, axis=0, keepdims=True)
    shift_grad = jnp.sum(grad, axis=0, keepdims=True)
    return back, gain_grad, shift_grad


def head_masks():
    head = lax.broadcasted_iota(jnp.int32, (SLOT, 256), 1) // HEAD_DIM
    return [[head == 0, head == 1, head == 2], [head == 1, head == 2, head == 3]]


def stack_heads(values, masks):
    zero = jnp.zeros_like(values)
    return jnp.concatenate([jnp.where(mask, values, zero) for mask in masks], axis=0)


def unstack_heads(values, masks):
    parts = [values[SLOT * i : SLOT * (i + 1)] for i in range(3)]
    return sum(jnp.where(mask, part, 0.0) for mask, part in zip(masks, parts))


def put_heads(ref, rows, start, first, second):
    ref[rows, start : start + 128] = first[:, :128].astype(BF16)
    ref[rows, start + 128 : start + 256] = (first[:, 128:] + second[:, :128]).astype(BF16)
    ref[rows, start + 256 : start + 384] = second[:, 128:].astype(BF16)


def attend(count_of, qkv, half, out, probs, scale, images):
    def one_image(image, carry):
        rows = rows_of(image, SLOT)
        live = lax.broadcasted_iota(jnp.int32, (SLOT, 3 * SLOT), 0) < count_of(image)
        parts = []
        for group, masks in enumerate(head_masks()):
            at = 128 * group
            query = qkv[half, rows, at : at + 256]
            key = qkv[half, rows, 384 + at : 384 + at + 256]
            value = qkv[half, rows, 768 + at : 768 + at + 256]
            scores = dot(key, stack_heads(query, masks), NT) * scale
            scores = jnp.where(live, scores, -1e9)
            top = jnp.max(scores, axis=0, keepdims=True)
            powers = jnp.exp(scores - top)
            weights = (powers / jnp.sum(powers, axis=0, keepdims=True)).astype(BF16)
            probs[rows_of((half * 16 + image) * 2 + group, SLOT), :] = weights
            parts.append(unstack_heads(dot(weights, value, TN), masks))
        put_heads(out, rows, half * 384, *parts)
        return carry

    lax.fori_loop(*images, one_image, 0, unroll=8)


def attend_back(qkv, half, out_grad, probs, scale, images):
    def one_image(image, carry):
        rows = rows_of(image, SLOT)
        queries, keys, values = [], [], []
        for group, masks in enumerate(head_masks()):
            at = 128 * group
            query = stack_heads(qkv[half, rows, at : at + 256], masks)
            key = qkv[half, rows, 384 + at : 384 + at + 256]
            value = qkv[half, rows, 768 + at : 768 + at + 256]
            grad = out_grad[rows, half * 384 + at : half * 384 + at + 256]
            grad = stack_heads(grad, masks)
            low = probs[rows_of((half * 16 + image) * 2 + group, SLOT), :]
            weights = low.astype(F32)
            prob_grad = dot(value, grad, NT)
            delta = jnp.sum(prob_grad * weights, axis=0, keepdims=True)
            score_grad = (weights * (prob_grad - delta)).astype(BF16)
            values.append(dot(low, grad, NN))
            keys.append(dot(score_grad, query, NN) * scale)
            queries.append(unstack_heads(dot(score_grad, key, TN), masks) * scale)
        put_heads(qkv.at[half], rows, 0, *queries)
        put_heads(qkv.at[half], rows, 384, *keys)
        put_heads(qkv.at[half], rows, 768, *values)
        return carry

    lax.fori_loop(*images, one_image, 0, unroll=8)


class Gather:
    def __init__(self, own, other, place, send, recv):
        self.place, self.send, self.recv = place, send, recv
        tensor, inner, outer = place.at
        whole = not place.split
        self.hop_y = self.copy(own(inner, whole), other(inner, whole), 0, place.over_y)
        self.hops = [self.hop_y]
        if place.split:
            across = lax.rem(inner + 2, 4)
            mine, theirs = other(inner, False), other(across, False)
            self.hop_x = self.copy(mine, mine, 1, place.over_x)
            self.hop_c = self.copy(mine, mine, 2, place.over_core)
            self.hop_xc = self.copy(theirs, theirs, 3, place.over_core)
            self.hops += [self.hop_x, self.hop_c, self.hop_xc]

    def copy(self, src, dst, kind, device):
        return pltpu.make_async_remote_copy(
            src_ref=src,
            dst_ref=dst,
            send_sem=self.send.at[kind],
            recv_sem=self.recv.at[kind],
            device_id=device,
            device_id_type=MESH,
        )

    def first(self):
        self.hop_y.start()

    def second(self):
        self.hop_y.wait_recv()
        if self.place.split:
            self.hop_x.start()
            self.hop_c.start()

    def third(self):
        if self.place.split:
            self.hop_x.wait_recv()
            self.hop_xc.start()

    def ready(self):
        if self.place.split:
            self.hop_c.wait_recv()
            self.hop_xc.wait_recv()

    def sent(self):
        self.hop_y.wait_send()
        self.handed_on()

    def handed_on(self):
        for hop in self.hops[1:]:
            hop.wait_send()


class Place:
    def __init__(self, split):
        self.split = split
        tensor, inner, outer = (lax.axis_index(a) for a in ("tensor", "inner", "outer"))
        self.at = (tensor, inner, outer)
        self.over_y = (1 - tensor, inner, outer)
        if split:
            core = lax.rem(inner, 2)
            self.over_x = (tensor, lax.rem(inner + 2, 4), outer)
            self.over_core = (tensor, inner + 1 - 2 * core, outer)

    def meet(self):
        partners = [self.over_y]
        if self.split:
            partners += [self.over_x, self.over_core]
        barrier = pltpu.get_barrier_semaphore()
        for device in partners:
            pl.semaphore_signal(barrier, inc=1, device_id=device, device_id_type=MESH)
        pl.semaphore_wait(barrier, len(partners))


def row_part(ref, lead, total, count):
    def part(index, whole):
        if whole:
            return ref.at[(*lead, pl.ds(0, total))]
        size = total // count
        return ref.at[(*lead, rows_of(index, size))]

    return part


def layer_kernel(
    split,
    counts,
    tokens,
    cotangent,
    gain1_ref,
    shift1_ref,
    out_bias_ref,
    gain2_ref,
    shift2_ref,
    down_bias_ref,
    qv_bias,
    up_bias,
    qkv_weight,
    out_weight,
    up_weight,
    down_weight,
    mixed,
    tokens_grad,
    gqkv,
    gout,
    gup,
    gdown,
    vectors,
    qv_sum,
    up_sum,
    staged,
    wqkv,
    wout,
    wup,
    wdown,
    biases,
    x_rows,
    gm,
    h1,
    qkv,
    att,
    probs,
    mid,
    h2,
    acc_y,
    acc_g,
    act,
    act_grad,
    mixed_part,
    sems,
    out_sems,
    send,
    recv,
):
    total, width = x_rows.shape
    quarter = total // QUAD
    slots, images = tokens.shape[:2]
    half_width = qkv_weight.shape[2]
    scale = HEAD_DIM**-0.5
    place = Place(split)
    mine = place.at[0]

    def count_of(image):
        return counts[mine, image]

    def line(ref):
        return ref[...].reshape(1, width)

    loads = [
        pltpu.make_async_copy(tokens, staged.at[pl.ds(0, slots)], sems.at[0]),
        pltpu.make_async_copy(qkv_weight, wqkv.at[0], sems.at[1]),
        pltpu.make_async_copy(out_weight, wout.at[0], sems.at[2]),
    ]
    for block in range(BLOCKS):
        for q in range(4):
            at = q * 384 + block * 128
            loads.append(
                pltpu.make_async_copy(
                    up_weight.at[:, pl.ds(at, 128)],
                    wup.at[block, :, pl.ds(q * 128, 128)],
                    sems.at[len(loads)],
                )
            )
            loads.append(
                pltpu.make_async_copy(
                    down_weight.at[pl.ds(at, 128)],
                    wdown.at[block, pl.ds(q * 128, 128)],
                    sems.at[len(loads)],
                )
            )
    for load in loads:
        load.start()
    pieces = []

    def piece(own, other):
        index = len(pieces)
        pieces.append(Gather(own, other, place, send.at[index], recv.at[index]))

    for part in range(3):
        piece(
            row_part(qkv_weight, (part,), width, 4), row_part(wqkv, (1, part), width, 4)
        )
    piece(row_part(out_weight, (), half_width, 4), row_part(wout, (1,), half_width, 4))
    for block in range(BLOCKS):
        piece(row_part(wup, (block,), width, 4), row_part(wup, (BLOCKS + block,), width, 4))
        piece(row_part(wdown, (block,), 512, 4), row_part(wdown, (BLOCKS + block,), 512, 4))
    biases[...] = jnp.zeros_like(biases)
    for block in range(BLOCKS):
        for q in range(4):
            at = q * 384 + block * 128
            found = up_bias[pl.ds(at, 128)].reshape(1, 128)
            biases[0, block : block + 1, q * 128 : (q + 1) * 128] = found
    biases[0, 3:5, :half_width] = qv_bias[...]
    place.meet()
    for gather in pieces[:4]:
        gather.first()
    bias_copy = pltpu.make_async_remote_copy(
        src_ref=biases.at[0],
        dst_ref=biases.at[1],
        send_sem=send.at[10, 0],
        recv_sem=recv.at[10, 0],
        device_id=place.over_y,
        device_id_type=MESH,
    )
    bias_copy.start()

    staged[slots:, :, :] = jnp.zeros((SLOT - slots, images, width), BF16)

    def by_image(target, masked):
        def some_slots(step, carry):
            values = staged[rows_of(step, 16)].astype(F32)
            values = jnp.swapaxes(values, 0, 1)
            for image in range(images):
                rows = pl.ds(pl.multiple_of(image * SLOT + step * 16, 16), 16)
                found = values[image]
                if masked:
                    slot = lax.broadcasted_iota(jnp.int32, (16, width), 0) + step * 16
                    found = jnp.where(slot < count_of(image), found, 0.0)
                target[rows, :] = found.astype(BF16)
            return carry

        lax.fori_loop(0, SLOT // 16, some_slots, 0)

    loads[0].wait()
    by_image(x_rows, False)
    load = pltpu.make_async_copy(cotangent, staged.at[pl.ds(0, slots)], sems.at[0])
    load.start()
    vectors[...] = jnp.zeros_like(vectors)
    gain1, shift1, gain2, shift2 = (
        line(r) for r in (gain1_ref, shift1_ref, gain2_ref, shift2_ref)
    )
    out_bias, down_bias = line(out_bias_ref), line(down_bias_ref)

    def first_norm(group, carry):
        rows = rows_of(group, quarter)
        hat, _ = norm_stats(x_rows[rows, :].astype(F32))
        h1[rows, :] = (hat * gain1 + shift1).astype(BF16)
        return carry

    lax.fori_loop(0, QUAD, first_norm, 0)
    for later in loads[1:]:
        later.wait()
    for gather in pieces[4:]:
        gather.first()
    pieces[0].second()

    def project(half, part):
        found = dot(h1[...], wqkv[half, part], NN)
        if part != 1:
            row = 3 + part // 2
            found = found + biases[half, row : row + 1, :half_width]
        qkv[half, :, 384 * part : 384 * (part + 1)] = found.astype(BF16)

    for part in range(3):
        project(0, part)
    pieces[1].second()
    attend(count_of, qkv, 0, att, probs, scale, (0, 8))
    pieces[2].second()
    pieces[0].third()
    load.wait()
    by_image(gm, True)
    pieces[1].third()
    attend(count_of, qkv, 0, att, probs, scale, (8, 16))
    pieces[3].second()
    pieces[2].third()
    bias_copy.wait()
    for part in range(3):
        pieces[part].ready()
        project(1, part)
    pieces[3].third()
    pieces[4].second()
    attend(count_of, qkv, 1, att, probs, scale, (0, 8))
    pieces[5].second()
    pieces[4].third()
    attend(count_of, qkv, 1, att, probs, scale, (8, 16))
    pieces[3].ready()

    for part in range(2):
        cols = slice(384 * part, 384 * (part + 1))
        weight = wout[:, :, cols].reshape(width, 384)
        mid[:, cols] = (
            x_rows[:, cols].astype(F32) + dot(att[...], weight, NN) + out_bias[:, cols]
        )

    def second_norm(group, carry):
        rows = rows_of(group, quarter)
        hat, _ = norm_stats(mid[rows, :])
        h2[rows, :] = (hat * gain2 + shift2).astype(BF16)
        vectors[5:6, :] += jnp.sum(gm[rows, :].astype(F32), axis=0, keepdims=True)
        return carry

    lax.fori_loop(0, QUAD, second_norm, 0)
    pieces[6].second()
    pieces[5].third()

    hooks = {
        (0, 0): [pieces[7].second, pieces[6].third],
        (0, 1): [pieces[8].second, pieces[7].third],
        (1, 0): [pieces[9].second, pieces[8].third],
        (1, 1): [pieces[9].third],
    }
    for order in range(2 * BLOCKS):
        half, block = order % 2, order // 2
        index = half * BLOCKS + block
        bias = biases[half, block : block + 1, :]
        if half == 1:
            pieces[4 + 2 * block].ready()
            pieces[5 + 2 * block].ready()

        def hidden(group, carry, index=index, bias=bias):
            rows = rows_of(group, quarter)
            u = dot(h2[rows, :], wup[index], NN) + bias
            cdf = 0.5 * (1.0 + lax.erf(u * 0.7071067811865476))
            act[rows, :] = (u * cdf).astype(BF16)
            slope = cdf + u * jnp.exp(-0.5 * u * u) * 0.3989422804014327
            low = (dot(gm[rows, :], wdown[index], NT) * slope).astype(BF16)
            act_grad[rows, :] = low
            return carry + jnp.sum(low.astype(F32), axis=0, keepdims=True)

        up_sum[index : index + 1, :] = lax.fori_loop(
            0, QUAD, hidden, jnp.zeros((1, 512), F32)
        )
        for step in hooks.get((order, 0), ()):
            step()
        for part in range(2):
            cols = slice(384 * part, 384 * (part + 1))
            y = dot(act[...], wdown[index, :, cols], NN)
            g = dot(act_grad[...], wup[index, cols, :], NT)
            if order == 0:
                acc_y[:, cols] = y
                acc_g[:, cols] = g
            else:
                acc_y[:, cols] += y
                acc_g[:, cols] += g
        for step in hooks.get((order, 1), ()):
            step()
        if half == 1:
            pieces[4 + 2 * block].handed_on()
            pieces[5 + 2 * block].handed_on()
        gup_now = dot(h2[...], act_grad[...], TN).astype(BF16)
        gdown_now = dot(act[...], gm[...], TN).astype(BF16)
        if half == 0:
            pieces[4 + 2 * block].hop_y.wait_send()
            pieces[5 + 2 * block].hop_y.wait_send()
        wup[index] = gup_now
        wdown[index] = gdown_now

    copies = [
        pltpu.make_async_copy(wup, gup, out_sems.at[0]),
        pltpu.make_async_copy(wdown, gdown, out_sems.at[1]),
    ]
    for copy in copies:
        copy.start()

    def ship(group):
        slot = lax.rem(group, 2)
        return pltpu.make_async_copy(
            mixed_part.at[slot], mixed.at[rows_of(group, quarter)], out_sems.at[2 + slot]
        )

    def finish(group, carry):
        rows = rows_of(group, quarter)

        @pl.when(group >= 2)
        def _():
            ship(group - 2).wait()

        values = mid[rows, :]
        mixed_part[lax.rem(group, 2)] = (values + acc_y[rows, :] + down_bias).astype(BF16)
        ship(group).start()
        back, gain_grad, shift_grad = norm_back(acc_g[rows, :], values, gain2)
        grad = gm[rows, :].astype(F32) + back
        acc_g[rows, :] = grad
        gm[rows, :] = grad.astype(BF16)
        vectors[2:3, :] += jnp.sum(grad, axis=0, keepdims=True)
        vectors[3:4, :] += gain_grad
        vectors[4:5, :] += shift_grad
        return carry

    lax.fori_loop(0, QUAD, finish, 0)
    for group in (QUAD - 2, QUAD - 1):
        ship(jnp.int32(group)).wait()

    out_grad = h2
    for half in range(2):
        cols = slice(384 * half, 384 * (half + 1))
        out_grad[:, cols] = dot(gm[...], wout[half], NT).astype(BF16)
    pieces[3].sent()
    for half in range(2):
        cols = slice(384 * half, 384 * (half + 1))
        wout[half] = dot(att[:, cols], gm[...], TN).astype(BF16)
    copies.append(pltpu.make_async_copy(wout, gout, out_sems.at[4]))
    copies[-1].start()
    copies[0].wait()

    for half in (1, 0):
        attend_back(qkv, half, out_grad, probs, scale, (0, 16))
        for part in range(3):
            cols = slice(384 * part, 384 * (part + 1))
            grads = qkv[half, :, cols]
            wup[3 * half + part, :, :384] = dot(h1[...], grads, TN).astype(BF16)
            if part != 1:
                at = 2 * half + part // 2
                qv_sum[at : at + 1, :] = jnp.sum(grads.astype(F32), axis=0, keepdims=True)
            index = 5 + 3 * half + part
            copies.append(
                pltpu.make_async_copy(
                    wup.at[3 * half + part, :, pl.ds(0, 384)],
                    gqkv.at[half, part],
                    out_sems.at[index],
                )
            )
            copies[-1].start()

    def last_norm(group, carry):
        rows = rows_of(group, quarter)
        grad = None
        for half in range(2):
            for part in range(3):
                cols = slice(384 * part, 384 * (part + 1))
                term = dot(qkv[half, rows, cols], wqkv[half, part], NT)
                grad = term if grad is None else grad + term
        values = x_rows[rows, :].astype(F32)
        back, gain_grad, shift_grad = norm_back(grad, values, gain1)
        acc_g[rows, :] += back
        vectors[0:1, :] += gain_grad
        vectors[1:2, :] += shift_grad
        return carry

    lax.fori_loop(0, QUAD, last_norm, 0)
    copies.append(pltpu.make_async_copy(acc_g, tokens_grad, out_sems.at[11]))
    copies[-1].start()
    for copy in copies[1:]:
        copy.wait()
    for gather in pieces[:3]:
        gather.sent()


def run_layer(split, *operands):
    tokens, qkv_weight = operands[1], operands[11]
    slots, images, width = tokens.shape
    total = images * SLOT
    half = qkv_weight.shape[2]
    vmem = pl.BlockSpec(memory_space=pltpu.VMEM)
    anywhere = pl.BlockSpec(memory_space=pl.ANY)
    shape = jax.ShapeDtypeStruct
    return pl.pallas_call(
        functools.partial(layer_kernel, split),
        out_shape=[
            shape((total, width), BF16),
            shape((total, width), F32),
            shape((2, 3, width, half), BF16),
            shape((2, half, width), BF16),
            shape((2 * BLOCKS, width, 512), BF16),
            shape((2 * BLOCKS, 512, width), BF16),
            shape((8, width), F32),
            shape((4, half), F32),
            shape((2 * BLOCKS, 512), F32),
        ],
        in_specs=[pl.BlockSpec(memory_space=pltpu.SMEM)]
        + [anywhere] * 2
        + [vmem] * 8
        + [anywhere] * 4,
        out_specs=[anywhere] * 6 + [vmem] * 3,
        scratch_shapes=[
            pltpu.VMEM((SLOT, images, width), BF16),
            pltpu.VMEM((2, 3, width, half), BF16),
            pltpu.VMEM((2, half, width), BF16),
            pltpu.VMEM((2 * BLOCKS, width, 512), BF16),
            pltpu.VMEM((2 * BLOCKS, 512, width), BF16),
            pltpu.VMEM((2, 8, 512), F32),
            pltpu.VMEM((total, width), BF16),
            pltpu.VMEM((total, width), BF16),
            pltpu.VMEM((total, width), BF16),
            pltpu.VMEM((2, total, 3 * half), BF16),
            pltpu.VMEM((total, width), BF16),
            pltpu.VMEM((4 * images * SLOT, 3 * SLOT), BF16),
            pltpu.VMEM((total, width), F32),
            pltpu.VMEM((total, width), BF16),
            pltpu.VMEM((total, width), F32),
            pltpu.VMEM((total, width), F32),
            pltpu.VMEM((total, 512), BF16),
            pltpu.VMEM((total, 512), BF16),
            pltpu.VMEM((2, total // QUAD, width), BF16),
            pltpu.SemaphoreType.DMA((3 + 8 * BLOCKS,)),
            pltpu.SemaphoreType.DMA((12,)),
            pltpu.SemaphoreType.DMA((11, 4)),
            pltpu.SemaphoreType.DMA((11, 4)),
        ],
        compiler_params=pltpu.CompilerParams(
            collective_id=0, has_side_effects=True, vmem_limit_bytes=64 * 2**20 - 2**17
        ),
    )(*operands)


def local(
    tokens,
    counts,
    norm1_gain,
    norm1_shift,
    qkv_weight,
    qv_bias,
    out_weight,
    out_bias,
    norm2_gain,
    norm2_shift,
    up_weight,
    up_bias,
    down_weight,
    down_bias,
    cotangent,
):
    images, slots, width = tokens.shape
    inner = lax.axis_size("inner")
    head_width = qkv_weight.shape[2]
    hidden = up_weight.shape[1]
    mixed, tokens_grad, gqkv, gout, gup, gdown, vectors, qv_sum, up_sum = run_layer(
        inner == 4,
        counts,
        tokens.transpose(1, 0, 2),
        cotangent.transpose(1, 0, 2),
        norm1_gain,
        norm1_shift,
        out_bias,
        norm2_gain,
        norm2_shift,
        down_bias,
        qv_bias,
        up_bias,
        qkv_weight.transpose(1, 0, 2),
        out_weight,
        up_weight,
        down_weight,
    )
    mixed = mixed.reshape(images, SLOT, width)[:, :slots]
    tokens_grad = tokens_grad.reshape(images, SLOT, width)[:, :slots]

    def own_half(grads):
        other = lax.ppermute(grads[1].astype(BF16), "tensor", [(0, 1), (1, 0)])
        return (grads[0].astype(F32) + other.astype(F32)).astype(BF16)

    gqkv = own_half(gqkv).transpose(1, 0, 2)
    gout = own_half(gout)
    back = lambda v: v.reshape(BLOCKS, width, 4, 128).transpose(1, 2, 0, 3).reshape(width, hidden)
    gup = back(own_half(gup.reshape(2, BLOCKS, width, 512)))
    gdown = own_half(gdown.reshape(2, BLOCKS, 512, width))
    gdown = gdown.reshape(BLOCKS, 4, 128, width).transpose(1, 0, 2, 3).reshape(hidden, width)
    qv_sum = own_half(qv_sum.reshape(2, 2, head_width))
    up_sum = own_half(up_sum.reshape(2, BLOCKS, 512))
    up_sum = up_sum.reshape(BLOCKS, 4, 128).transpose(1, 0, 2).reshape(hidden)
    vectors = lax.psum(vectors.astype(BF16), "tensor")

    def reduce(grads, dim=0):
        part = lax.psum_scatter(grads, "inner", scatter_dimension=dim, tiled=True)
        return lax.psum(part, "outer").astype(F32)

    gqkv = reduce(gqkv)
    gout = reduce(gout)
    gup = reduce(gup)
    gdown = reduce(gdown)
    vectors = reduce(vectors.T)
    qv_sum = reduce(qv_sum.T).T
    up_sum = reduce(up_sum)
    return (
        mixed,
        tokens_grad,
        vectors[:, 0],
        vectors[:, 1],
        gqkv,
        qv_sum,
        gout,
        vectors[:, 2],
        vectors[:, 3],
        vectors[:, 4],
        gup,
        up_sum,
        gdown,
        vectors[:, 5],
    )


def solution(mesh):
    in_specs = (
        P(("tensor", "inner", "outer"), None, None),
        P(None, ("inner", "outer")),
        P(),
        P(),
        P(None, None, "tensor"),
        P(None, "tensor"),
        P("tensor", None),
        P(),
        P(),
        P(),
        P(None, "tensor"),
        P("tensor"),
        P("tensor", None),
        P(),
        P(("tensor", "inner", "outer"), None, None),
    )
    out_specs = (
        P(("tensor", "inner", "outer"), None, None),
        P(("tensor", "inner", "outer"), None, None),
        P("inner"),
        P("inner"),
        P("inner", None, "tensor"),
        P(None, ("tensor", "inner")),
        P(("tensor", "inner"), None),
        P("inner"),
        P("inner"),
        P("inner"),
        P("inner", "tensor"),
        P(("tensor", "inner")),
        P(("tensor", "inner"), None),
        P("inner"),
    )
    return jax.shard_map(local, mesh=mesh, in_specs=in_specs, out_specs=out_specs, check_vma=False)
```

time: 704 us -> 505 us (0.72)
  waiting for transfers between devices: 416 us -> 265 us
  local copies, waits for them, and re-layouts: 74.8 us -> 35 us
  Pallas kernels: 123 us -> 144 us
  other arithmetic: 27 us -> 11.9 us
  starting transfers between devices: 16.8 us -> 5.73 us
    ppermute x6 -> x0, waiting for transfers between devices: 130 us -> none  [both(): other = lax.ppermute(own, 'tensor', [(0, 1), (1, 0)])]
    pallas_call x1, Pallas kernels: 123 us -> 144 us  [run_layer(): pl.pallas_call(functools.partial(layer_kernel, split), out_shape=[shape((...]
    another operation x6 -> x0, other arithmetic: 16.6 us -> none  [both(): return jnp.stack([own, other])]
    unnamed x52 -> x31, local copies, waits for them, and re-layouts: 31.8 us -> 19.7 us
    reduce_scatter x3, waiting for transfers between devices: 36.7 us -> 26 us  [reduce(): part = lax.psum_scatter(grads, 'inner', scatter_dimension=dim, tiled=True)]
    reshape x10 -> x0, local copies, waits for them, and re-layouts: 9.17 us -> none  [the longest x6 3.52 us: local(): v.reshape(1, width)]
    transpose x3 -> x1, local copies, waits for them, and re-layouts: 10.4 us -> 1.59 us  [local(): gdown.reshape(BLOCKS, 4, 128, width).transpose(1, 0, 2, 3)]
    ppermute x6 -> x0, starting transfers between devices: 8.83 us -> none  [both(): other = lax.ppermute(own, 'tensor', [(0, 1), (1, 0)])]
  transfers between devices with their start and end apart: 19 -> 13, of which waited for: 11 -> 8; matrix products, arithmetic and copies ran while one was open for 12% -> 6% of each run, Pallas kernels for 0% -> 0%
where the time goes in v2:
time: 505 us; the launch traced here: 500 us
  waiting for transfers between devices  265 us (52%)
  Pallas kernels  144 us (29%)
  local copies, waits for them, and re-layouts  35 us (7%)
  blocking collectives  23.3 us (5%)
  between operations  15.5 us (3%)
  other arithmetic  11.9 us (2%)
  starting transfers between devices  5.73 us (1%)
    ppermute x6, waiting for transfers between devices, own_half(): other = lax.ppermute(grads[1].astype(BF16), 'tensor', [(0, 1), (1, 0)])  144 us
    pallas_call x1, Pallas kernels, run_layer(): pl.pallas_call(functools.partial(layer_kernel, split), out_shape=[shape((...  144 us
    psum x1, waiting for transfers between devices, reduce(): return lax.psum(part, 'outer').astype(F32)  66.8 us
    unnamed x10, waiting for transfers between devices  27.7 us
    reduce_scatter x3, waiting for transfers between devices, reduce(): part = lax.psum_scatter(grads, 'inner', scatter_dimension=dim, tiled=True)  26 us
    unnamed x31, local copies, waits for them, and re-layouts  19.7 us
    psum x1, blocking collectives, reduce(): return lax.psum(part, 'outer').astype(F32)  12.4 us
  transfers between devices with their start and end apart: 13, of which 8 were waited for; matrix products, arithmetic and copies ran while one was open for 6% of the time, Pallas kernels for 0%

profile of v2, /device:TPU:0, one launch (start us, length us, event | category | flops | bytes accessed | tf_op | source)
XLA Modules:
  0.0 500.0 jit_solution(10580251690785338520)
XLA Ops:
  7.2 0.0 reduce-scatter.21.cloned.1.call-start
  7.2 143.7 %shard_map.254 = (bf16[1280,768]{1,0:T(8,128)(2,1)}, f32[1280,768]{1,0:T(8,128)}, bf16[2,3,768,384]{3,2,1,0:T(8,128)(2,1)}, bf16[2,384,768]{2,1,0:T(8,128)(2,1)}...) custom-call(s32[2,16]{1,0:T(2,128)} %counts.1, ...), custom_call_target="tpu_custom_call" | custom-call | tf_op jit(solution)/shard_map/pallas_call | solution.py:567
  151.0 0.0 copy-start
  151.0 2.0 slice.84
  153.0 0.1 collective-permute-start.3
  153.0 48.9 %collective-permute-done.3 = bf16[3,768,512]{2,1,0:T(8,128)(2,1)S(1)} collective-permute-done((bf16[3,768,512]{2,1,0:T(8,128)(2,1)S(1)}, bf16[3,768,512]{2,1,0:T(8,128)(2,1)S(1)}, u32[]{:S(2)}, u32[]{:S(2)}) %collective-permute-start.3) | collective-permute-done | bytes 2359328 | tf_op jit(solution)/shard_map/ppermute | solution.py:659
  202.0 0.7 add_convert_fusion.1
  202.6 2.1 reshape.78
  204.8 4.1 copy.41
  208.9 2.4 copy.47
  211.3 0.0 reduce-scatter.21.cloned.1.call-update
  211.3 0.0 reduce-scatter.15.cloned.1.call-start
  211.4 3.0 slice_bitcast_fusion
  214.4 0.3 collective-permute-start
  214.7 1.8 collective-permute-start.2
  216.5 46.1 %collective-permute-done.2 = bf16[384,768]{1,0:T(8,128)(2,1)S(1)} collective-permute-done((bf16[384,768]{1,0:T(8,128)(2,1)S(1)}, bf16[384,768]{1,0:T(8,128)(2,1)S(1)}, u32[]{:S(2)}, u32[]{:S(2)}) %collective-permute-start.2) | collective-permute-done | bytes 589856 | tf_op jit(solution)/shard_map/ppermute | solution.py:659
  262.6 1.0 fusion.2
  263.6 0.0 reduce-scatter.15.cloned.1.call-update
  263.6 0.0 reduce-scatter.13.cloned.1.call-start
  263.6 0.0 collective-permute-done
  263.7 3.1 fusion.1
  266.8 0.0 reduce-scatter.13.cloned.1.call-update
  266.8 0.0 reduce-scatter.17.cloned.1.call-start
  266.8 1.8 slice.88
  268.7 0.6 collective-permute-start.5
  269.3 46.5 %collective-permute-done.5 = bf16[3,512,768]{2,1,0:T(8,128)(2,1)S(1)} collective-permute-done((bf16[3,512,768]{2,1,0:T(8,128)(2,1)S(1)}, bf16[3,512,768]{2,1,0:T(8,128)(2,1)S(1)}, u32[]{:S(2)}, u32[]{:S(2)}) %collective-permute-start.5) | collective-permute-done | bytes 2359328 | tf_op jit(solution)/shard_map/ppermute | solution.py:659
  315.8 2.2 add_convert_fusion
  318.1 1.6 copy.43
  319.7 0.0 reduce-scatter.17.cloned.1.call-update
  319.7 0.0 reduce-scatter.19.cloned.1.call-start
  319.8 0.6 copy-done.8
  320.4 0.8 collective-permute-start.1
  321.2 2.8 collective-permute-done.1
  323.9 0.8 copy.45
  324.8 0.0 reduce-scatter.19.cloned.1.call-update
  324.8 0.0 reduce-scatter.23.cloned.1.call-start
  324.8 0.8 copy.49
  325.7 0.0 reduce-scatter.23.cloned.1.call-update
  325.7 0.3 all-reduce.5.cloned.1.call-start
  326.0 0.0 reduce-scatter.21.cloned.1.call-done
  326.1 2.3 copy.48
  328.3 26.0 %reduce-scatter.17.cloned.1.call-done = bf16[384,768]{1,0:T(8,128)(2,1)} async-done(((bf16[1536,768]{1,0:T(8,128)(2,1)}), bf16[384,768]{1,0:T(8,128)(2,1)}) %reduce-scatter.17.cloned.1.call-update) | async-done | bytes 589840 | tf_op jit(solution)/shard_map/reduce_scatter | solution.py:674
  354.4 0.0 all-reduce.5.cloned.1.call-update
  354.4 1.6 collective-permute-start.4
  356.0 1.8 copy.51
  357.8 6.2 %copy.52 = f32[16,78,768]{2,0,1:T(8,128)} copy(f32[16,78,768]{2,1,0:T(8,128)} %bitcast.48) | data formatting | bytes 7667712
  364.0 0.6 dynamic-slice
  365.3 0.0 collective-permute-done.4
  365.3 6.0 %all-reduce = bf16[1536]{0:T(1024)(128)(2,1)S(1)} all-reduce(bf16[1536]{0:T(1024)(128)(2,1)S(1)} %reshape.81), channel_id=7, replica_groups=mesh['tensor'=2,'inner'=4,'outer'=4] {'inner'}, use_global_device_ids=true, to_apply=%region_11.0.clone | all-reduce | flops 1536 | bytes 6144
  371.3 0.1 dynamic-slice.1
  371.4 5.6 %reduce-scatter.19.cloned.1.call-done = bf16[96,2]{1,0:T(8,128)(2,1)} async-done(((bf16[384,2]{1,0:T(8,128)(2,1)}), bf16[96,2]{1,0:T(8,128)(2,1)}) %reduce-scatter.19.cloned.1.call-update) | async-done | bytes 400
  376.9 0.8 copy.46
  377.7 22.0 %reduce-scatter.23.cloned.1.call-done = bf16[192,8]{1,0:T(8,128)(2,1)} async-done(((bf16[768,8]{1,0:T(8,128)(2,1)}), bf16[192,8]{1,0:T(8,128)(2,1)}) %reduce-scatter.23.cloned.1.call-update) | async-done | bytes 3088
  399.7 0.8 copy.50
  400.6 4.9 psum.64
  405.5 12.4 %all-reduce.1 = (bf16[192,8]{0,1:T(8,128)(2,1)S(1)}, bf16[2,96]{1,0:T(2,128)(2,1)S(1)}, bf16[384]{0:T(512)(128)(2,1)S(1)}) all-reduce(bf16[192,8]{0,1:T(8,128)(2,1)S(1)} %psum.64, bf16[2,96]{1,0:T(2,128)(2,1)S(1)} %bitcast.53, bf16[384]{0:T(512)(128)(2,1)S(1)} %dynamic-slice.1), channel_id=1, replica_groups=mesh['tensor'=2,'inner'=4,'outer'=4] {'outer'}, use_global_device_ids=true, to_apply=%region_2.0 | all-reduce | flops 2112 | bytes 8448 | tf_op jit(solution)/shard_map/psum | solution.py:675
  417.9 0.6 transpose.40
  418.5 0.6 convert_element_type.98
  419.1 0.6 fusion.5
  419.7 66.8 %all-reduce.5.cloned.1.call-done = (bf16[192,1536]{0,1:T(8,128)(2,1)}, bf16[192,3,384]{2,0,1:T(8,128)(2,1)}, bf16[96,768]{1,0:T(8,128)(2,1)}, bf16[384,768]{1,0:T(8,128)(2,1)}) async-done(((bf16[192,1536]{0,1:T(8,128)(2,1)}, bf16[192,3,384]{2,0,1:T(8,128)(2,1)}, bf16[96,768]{1,0:T(8,128)(2,1)}, bf16[384,768]{1,0:T(8,128)(2,1)}), (bf16[192,1536]{0,1:T(8,128)(2,1)}, bf16[192,3,384]{2,0,1:T(8,128)(2,1)}, ...) | async-done | bytes 1769488 | tf_op jit(solution)/shard_map/psum | solution.py:675
  486.4 1.7 convert_element_type.91
  488.2 2.4 copy.44
  490.6 1.0 convert_element_type.84
  491.6 1.1 convert_element_type.102
  (27 shorter events, 0.1 us)
Async XLA Ops:
  7.2 318.9 %reduce-scatter.21.cloned.1.call-start = ((), (), s32[]{:S(2)}) async-start(), calls=%async_computation.10 | async-start | bytes 2949120
  151.0 51.0 %copy-start = (bf16[6,768,512]{2,1,0:T(8,128)(2,1)S(1)}, bf16[6,768,512]{2,1,0:T(8,128)(2,1)}, u32[]{:S(2)}) copy-start(bf16[6,768,512]{2,1,0:T(8,128)(2,1)} %get-tuple-element.29) | copy-start | bytes 14155780
  153.0 49.0 %collective-permute-start.3 = (bf16[3,768,512]{2,1,0:T(8,128)(2,1)S(1)}, bf16[3,768,512]{2,1,0:T(8,128)(2,1)S(1)}, u32[]{:S(2)}, u32[]{:S(2)}) collective-permute-start(bf16[3,768,512]{2,1,0:T(8,128)(2,1)S(1)} %slice.84), channel_id=1, source_target_pairs={{0,16},{16,0},{1,17},{17,1},{2,18},{18,2},{3,19},{19,3},{4,20},{20... | collective-permute-start | bytes 7077896 | tf_op jit(solution)/shard_map/ppermute | solution.py:659
  211.3 117.0 %reduce-scatter.15.cloned.1.call-start = ((), (), s32[]{:S(2)}) async-start(), calls=%async_computation.7 | async-start | bytes 737280 | tf_op jit(solution)/shard_map/reduce_scatter | solution.py:674
  211.4 3.3 copy-start.3
  214.4 49.3 %copy-start.1 = (bf16[2,3,768,384]{3,2,1,0:T(8,128)(2,1)S(1)}, bf16[2,3,768,384]{3,2,1,0:T(8,128)(2,1)}, u32[]{:S(2)}) copy-start(bf16[2,3,768,384]{3,2,1,0:T(8,128)(2,1)} %get-tuple-element.26) | copy-start | bytes 10616836
  214.4 49.3 %collective-permute-start = (bf16[3,768,384]{2,1,0:T(8,128)(2,1)}, bf16[3,768,384]{2,1,0:T(8,128)(2,1)}, u32[]{:S(2)}, u32[]{:S(2)}) collective-permute-start(bf16[3,768,384]{2,1,0:T(8,128)(2,1)} %slice_bitcast_fusion), channel_id=1, source_target_pairs={{0,16},{16,0},{1,17},{17,1},{2,18},{18,2},{3,19},{19,3},{4,20},{20... | collective-permute-start | bytes 5308424 | tf_op jit(solution)/shard_map/ppermute | solution.py:659
  214.7 47.9 %collective-permute-start.2 = (bf16[384,768]{1,0:T(8,128)(2,1)S(1)}, bf16[384,768]{1,0:T(8,128)(2,1)S(1)}, u32[]{:S(2)}, u32[]{:S(2)}) collective-permute-start(bf16[384,768]{1,0:T(8,128)(2,1)S(1)} %slice_bitcast_fusion.1), channel_id=1, source_target_pairs={{0,16},{16,0},{1,17},{17,1},{2,18},{18,2},{3,19},{19,3},{4,20},{20... | collective-permute-start | bytes 1769480 | tf_op jit(solution)/shard_map/ppermute | solution.py:659
  263.6 64.7 %reduce-scatter.13.cloned.1.call-start = ((), (), s32[]{:S(2)}) async-start(), calls=%async_computation.6 | async-start | bytes 2211840 | tf_op jit(solution)/shard_map/reduce_scatter | solution.py:674
  266.8 87.6 %reduce-scatter.17.cloned.1.call-start = ((), (), s32[]{:S(2)}) async-start(), calls=%async_computation.8 | async-start | bytes 2949120 | tf_op jit(solution)/shard_map/reduce_scatter | solution.py:674
  268.7 47.2 %collective-permute-start.5 = (bf16[3,512,768]{2,1,0:T(8,128)(2,1)S(1)}, bf16[3,512,768]{2,1,0:T(8,128)(2,1)S(1)}, u32[]{:S(2)}, u32[]{:S(2)}) collective-permute-start(bf16[3,512,768]{2,1,0:T(8,128)(2,1)S(1)} %slice.88), channel_id=1, source_target_pairs={{0,16},{16,0},{1,17},{17,1},{2,18},{18,2},{3,19},{19,3},{4,20},{20... | collective-permute-start | bytes 7077896 | tf_op jit(solution)/shard_map/ppermute | solution.py:659
  319.7 0.7 copy-start.8
  319.7 5.2 %copy-start.6 = (f32[8,768]{1,0:T(8,128)S(1)}, f32[8,768]{1,0:T(8,128)}, u32[]{:S(2)}) copy-start(f32[8,768]{1,0:T(8,128)} %get-tuple-element.25) | copy-start | bytes 73732
  319.7 34.7 %copy-start.7 = (f32[6,512]{1,0:T(8,128)S(1)}, f32[6,512]{1,0:T(8,128)}, u32[]{:S(2)}) copy-start(f32[6,512]{1,0:T(8,128)} %get-tuple-element.30) | copy-start | bytes 36868
  319.7 36.3 %copy-start.2 = (bf16[1280,768]{1,0:T(8,128)(2,1)S(1)}, bf16[1280,768]{1,0:T(8,128)(2,1)}, u32[]{:S(2)}) copy-start(bf16[1280,768]{1,0:T(8,128)(2,1)} %get-tuple-element.23) | copy-start | bytes 5898244
  319.7 57.2 %reduce-scatter.19.cloned.1.call-start = ((), (), s32[]{:S(2)}) async-start(), calls=%async_computation.9 | async-start | bytes 122880
  320.4 3.6 collective-permute-start.1
  324.8 75.0 %reduce-scatter.23.cloned.1.call-start = ((), (), s32[]{:S(2)}) async-start(), calls=%async_computation.11 | async-start | bytes 245760
  325.7 160.8 %all-reduce.5.cloned.1.call-start = ((), (), s32[]{:S(2)}) async-start(), calls=%async_computation.12 | async-start | bytes 3932160 | tf_op jit(solution)/shard_map/psum | solution.py:675
  354.4 10.9 %collective-permute-start.4 = (bf16[3,512]{1,0:T(4,128)(2,1)S(1)}, bf16[3,512]{1,0:T(4,128)(2,1)S(1)}, u32[]{:S(2)}, u32[]{:S(2)}) collective-permute-start(bf16[3,512]{1,0:T(4,128)(2,1)S(1)} %slice.114), channel_id=1, source_target_pairs={{0,16},{16,0},{1,17},{17,1},{2,18},{18,2},{3,19},{19,3},{4,20},{20... | collective-permute-start | bytes 9224 | tf_op jit(solution)/shard_map/ppermute | solution.py:659
  357.8 6.2 %copy-start.9 = (u32[32]{0:T(128)S(1)}, u32[32]{0:T(128)}, u32[]{:S(2)}) copy-start(u32[32]{0:T(128)} %constant.4) | copy-start | bytes 388
  486.4 4.1 copy-start.5
  486.4 5.1 %copy-start.4 = (bf16[384,768]{1,0:T(8,128)(2,1)S(1)}, bf16[384,768]{1,0:T(8,128)(2,1)}, u32[]{:S(2)}) copy-start(bf16[384,768]{1,0:T(8,128)(2,1)} %get-tuple-element.66) | copy-start | bytes 1769476
Sparse Core Ops, SparseCore 0:
  211.5 33.2 reduce-scatter.20
  263.7 22.3 reduce-scatter.14
  289.5 29.3 reduce-scatter.12
  321.3 33.0 reduce-scatter.16
  357.3 19.5 reduce-scatter.18
  379.9 19.7 reduce-scatter.22
  403.1 83.2 all-reduce.4

commit v3 on v2

--- a/solution.py
+++ b/solution.py
@@ -181,15 +181,174 @@
             core = lax.rem(inner, 2)
             self.over_x = (tensor, lax.rem(inner + 2, 4), outer)
             self.over_core = (tensor, inner + 1 - 2 * core, outer)
+            self.over_z = [(tensor, inner, lax.rem(outer + step, 4)) for step in range(1, 4)]
 
     def meet(self):
         partners = [self.over_y]
         if self.split:
-            partners += [self.over_x, self.over_core]
+            partners += [self.over_x, self.over_core] + self.over_z
         barrier = pltpu.get_barrier_semaphore()
         for device in partners:
             pl.semaphore_signal(barrier, inc=1, device_id=device, device_id_type=MESH)
         pl.semaphore_wait(barrier, len(partners))
+
+
+def add_into(target, found):
+    target[...] = (target[...].astype(F32) + found[...].astype(F32)).astype(target.dtype)
+
+
+class Reduce:
+    CORE, X, Y, RS, AG = 0, 4, 6, 8, 11
+
+    def __init__(self, grads, size, place, send, recv, core, first, second, outer, x_first):
+        self.grads, self.size, self.place = grads, size, place
+        self.send, self.recv = send, recv
+        self.core, self.first, self.second, self.outer = core, first, second, outer
+        self.x_first = x_first
+        _, inner, self.z = place.at
+        self.c, self.x = lax.rem(inner, 2), inner // 2
+        self.inner = inner
+
+    def copy(self, src, dst, kind, device):
+        return pltpu.make_async_remote_copy(
+            src_ref=src,
+            dst_ref=dst,
+            send_sem=self.send.at[kind],
+            recv_sem=self.recv.at[kind],
+            device_id=device,
+            device_id_type=MESH,
+        )
+
+    def kept(self, half, across):
+        return self.grads(half, 2 * across + self.c)
+
+    def core_copies(self, half):
+        return [
+            self.copy(
+                self.grads(half, 2 * across + 1 - self.c),
+                self.core(half, across),
+                self.CORE + 2 * half + across,
+                self.place.over_core,
+            )
+            for across in range(2)
+        ]
+
+    def core_send(self, halves=(0, 1)):
+        for half in halves:
+            for copy in self.core_copies(half):
+                copy.start()
+
+    def core_add(self, halves=(0, 1)):
+        for half in halves:
+            for across, copy in enumerate(self.core_copies(half)):
+                copy.wait()
+                add_into(self.kept(half, across), self.core(half, across))
+
+    def x_copy(self, half):
+        target = self.first(half) if self.x_first else self.second()
+        source = self.kept(half, 1 - self.x)
+        return self.copy(source, target, self.X + half, self.place.over_x)
+
+    def x_send(self, halves=None):
+        for half in halves or ((0, 1) if self.x_first else (0,)):
+            self.x_copy(half).start()
+
+    def x_add(self, halves=None):
+        for half in halves or ((0, 1) if self.x_first else (0,)):
+            self.x_copy(half).wait()
+            add_into(self.kept(half, self.x), self.first(half) if self.x_first else self.second())
+
+    def y_copies(self):
+        if self.x_first:
+            sent = [(self.kept(1, self.x), self.second())]
+        else:
+            sent = [(self.kept(1, across), self.first(across)) for across in range(2)]
+        return [
+            self.copy(src, dst, self.Y + k, self.place.over_y) for k, (src, dst) in enumerate(sent)
+        ]
+
+    def y_send(self):
+        for copy in self.y_copies():
+            copy.start()
+
+    def y_add(self):
+        for across, copy in enumerate(self.y_copies()):
+            copy.wait()
+            if self.x_first:
+                add_into(self.kept(0, self.x), self.second())
+            else:
+                add_into(self.kept(0, across), self.first(across))
+
+    def mine(self):
+        return self.grads(0, self.inner)
+
+    def fourth(self, which):
+        size = self.size // 4
+        return self.grads(0, self.inner, pl.multiple_of(which * size, 16), size)
+
+    def rs_copies(self):
+        found = []
+        for step in range(1, 4):
+            there = lax.rem(self.z + step, 4)
+            device = (self.place.at[0], self.inner, there)
+            found.append(
+                self.copy(self.fourth(there), self.outer(step - 1), self.RS + step - 1, device)
+            )
+        return found
+
+    def rs_send(self):
+        for copy in self.rs_copies():
+            copy.start()
+
+    def rs_add(self):
+        for copy in self.rs_copies():
+            copy.wait()
+        total = self.fourth(self.z)[...].astype(F32)
+        for step in range(3):
+            total = total + self.outer(step)[...].astype(F32)
+        self.fourth(self.z)[...] = total.astype(BF16)
+
+    def ag_copies(self):
+        found = []
+        for step in range(1, 4):
+            device = (self.place.at[0], self.inner, lax.rem(self.z + step, 4))
+            part = self.fourth(self.z)
+            found.append(self.copy(part, self.outer(2 + step), self.AG + step - 1, device))
+        return found
+
+    def ag_send(self):
+        for copy in self.ag_copies():
+            copy.start()
+
+    def ag_wait(self):
+        for copy in self.ag_copies():
+            copy.wait()
+
+    def summed(self):
+        size = self.size // 4
+        found = [(self.fourth(self.z), self.z * size)]
+        for step in range(1, 4):
+            found.append((self.outer(2 + step), lax.rem(self.z + 4 - step, 4) * size))
+        return [(ref, pl.ds(pl.multiple_of(row, 16), size)) for ref, row in found]
+
+    def whole_copies(self):
+        found = []
+        for step in range(1, 4):
+            device = (self.place.at[0], self.inner, lax.rem(self.z + step, 4))
+            found.append(self.copy(self.mine(), self.outer(step - 1), self.RS + step - 1, device))
+        return found
+
+    def whole_send(self):
+        for copy in self.whole_copies():
+            copy.start()
+
+    def whole_add(self):
+        for copy in self.whole_copies():
+            copy.wait()
+        total = self.mine()[...].astype(F32)
+        for step in range(3):
+            total = total + self.outer(step)[...].astype(F32)
+        self.mine()[...] = total.astype(BF16)
 
 
 def row_part(ref, lead, total, count):
@@ -225,9 +384,7 @@
     gout,
     gup,
     gdown,
-    vectors,
-    qv_sum,
-    up_sum,
+    sums,
     staged,
     wqkv,
     wout,
@@ -251,10 +408,26 @@
     out_sems,
     send,
     recv,
+    core_up,
+    core_down,
+    first_up,
+    first_down,
+    second_up,
+    second_down,
+    outer_up,
+    outer_down,
+    out_parts,
+    sums_in,
+    sum_send,
+    sum_recv,
+    small_send,
+    small_recv,
+    credit,
 ):
     total, width = x_rows.shape
     quarter = total // QUAD
-    slots, images = tokens.shape[:2]
+    images = counts.shape[1]
+    slots = tokens.shape[0] // images
     half_width = qkv_weight.shape[2]
     scale = HEAD_DIM**-0.5
     place = Place(split)
@@ -267,7 +440,7 @@
         return ref[...].reshape(1, width)
 
     loads = [
-        pltpu.make_async_copy(tokens, staged.at[pl.ds(0, slots)], sems.at[0]),
+        pltpu.make_async_copy(tokens, staged.at[pl.ds(0, slots * images)], sems.at[0]),
         pltpu.make_async_copy(qkv_weight, wqkv.at[0], sems.at[1]),
         pltpu.make_async_copy(out_weight, wout.at[0], sems.at[2]),
     ]
@@ -324,11 +497,12 @@
     )
     bias_copy.start()
 
-    staged[slots:, :, :] = jnp.zeros((SLOT - slots, images, width), BF16)
+    staged[slots * images :, :] = jnp.zeros(((SLOT - slots) * images, width), BF16)
 
     def by_image(target, masked):
         def some_slots(step, carry):
-            values = staged[rows_of(step, 16)].astype(F32)
+            values = staged[rows_of(step, 16 * images), :].astype(F32)
+            values = values.reshape(16, images, width)
             values = jnp.swapaxes(values, 0, 1)
             for image in range(images):
                 rows = pl.ds(pl.multiple_of(image * SLOT + step * 16, 16), 16)
@@ -343,9 +517,9 @@
 
     loads[0].wait()
     by_image(x_rows, False)
-    load = pltpu.make_async_copy(cotangent, staged.at[pl.ds(0, slots)], sems.at[0])
+    load = pltpu.make_async_copy(cotangent, staged.at[pl.ds(0, slots * images)], sems.at[0])
     load.start()
-    vectors[...] = jnp.zeros_like(vectors)
+    sums[...] = jnp.zeros_like(sums)
     gain1, shift1, gain2, shift2 = (
         line(r) for r in (gain1_ref, shift1_ref, gain2_ref, shift2_ref)
     )
@@ -406,12 +580,179 @@
         rows = rows_of(group, quarter)
         hat, _ = norm_stats(mid[rows, :])
         h2[rows, :] = (hat * gain2 + shift2).astype(BF16)
-        vectors[5:6, :] += jnp.sum(gm[rows, :].astype(F32), axis=0, keepdims=True)
+        sums[1, 5:6, :] += jnp.sum(gm[rows, :].astype(F32), axis=0, keepdims=True)
         return carry
 
     lax.fori_loop(0, QUAD, second_norm, 0)
     pieces[6].second()
     pieces[5].third()
+
+    inner = place.at[1]
+
+    def up_part(block):
+        def part(half, q, start=0, size=192):
+            return wup.at[half * BLOCKS + block, pl.ds(pl.multiple_of(q * 192 + start, 16), size)]
+
+        return part
+
+    def down_part(block):
+        def part(half, q, start=0, size=128):
+            return wdown.at[half * BLOCKS + block, pl.ds(pl.multiple_of(q * 128 + start, 16), size)]
+
+        return part
+
+    def out_part(half, q, start=0, size=96):
+        return wout.at[half, pl.ds(pl.multiple_of(q * 96 + start, 16), size)]
+
+    homes = [
+        [(gm, 0), (gm, 384), (staged, 384)],
+        [(att, 0), (att, 384), (staged, 0)],
+    ]
+
+    def qkv_part(which):
+        def part(half, q, start=0, size=192):
+            ref, col = homes[half][which]
+            rows = pl.ds(pl.multiple_of(q * 192 + start, 16), size)
+            return ref.at[rows, pl.ds(col, 384)]
+
+        return part
+
+    spare = [
+        (ref, row, col) for ref in (att, gm, staged) for row in (768, 960) for col in (0, 384)
+    ] + [(ref, 192 * k, 0) for ref in (act, act_grad) for k in range(6)]
+
+    def taken(index):
+        ref, row, col = spare[index]
+        return ref.at[pl.ds(row, 192), pl.ds(col, 384)]
+
+    few = [
+        (ref, row, col) for ref in (att, gm, staged) for row in (1152, 1200) for col in (0, 384)
+    ] + [(ref, row, 0) for ref in (act, act_grad) for row in (1152, 1200)]
+
+    def taken_few(part, step):
+        if part == 2:
+            ref, row, col = act_grad, 576 + 48 * step, 0
+        else:
+            ref, row, col = few[6 * part + step]
+        return ref.at[pl.ds(row, 48), pl.ds(col, 384)]
+
+    ups, downs, qkvs = [], [], []
+    if split:
+        for block in range(BLOCKS):
+            ups.append(
+                Reduce(
+                    up_part(block), 192, place, sum_send.at[0], sum_recv.at[0],
+                    lambda half, across: core_up.at[half, across],
+                    lambda across: first_up.at[across],
+                    lambda: second_up,
+                    lambda step: outer_up.at[step],
+                    False,
+                )
+            )
+            downs.append(
+                Reduce(
+                    down_part(block), 128, place, sum_send.at[1], sum_recv.at[1],
+                    lambda half, across: core_down.at[half, across],
+                    lambda half: first_down.at[half],
+                    lambda: second_down,
+                    lambda step: outer_down.at[step],
+                    True,
+                )
+            )
+        outs = Reduce(
+            out_part, 96, place, sum_send.at[2], sum_recv.at[2],
+            lambda half, across: out_parts.at[2 * half + across],
+            lambda across: out_parts.at[4 + across],
+            lambda: out_parts.at[6],
+            lambda step: out_parts.at[7 + step],
+            False,
+        )
+        for part in range(3):
+            qkvs.append(
+                Reduce(
+                    qkv_part(part), 192, place, sum_send.at[3 + part], sum_recv.at[3 + part],
+                    lambda half, across, part=part: taken(4 * part + 2 * half + across),
+                    lambda half, part=part: taken(12 + 2 * part + half),
+                    lambda part=part: taken(18 + part),
+                    lambda step, part=part: taken_few(part, step),
+                    True,
+                )
+            )
+
+    def free(index, device):
+        pl.semaphore_signal(credit.at[index], inc=1, device_id=device, device_id_type=MESH)
+
+    def may(index, count=1):
+        pl.semaphore_wait(credit.at[index], count)
+
+    stores = []
+
+    def store(src, dst):
+        copy = pltpu.make_async_copy(src, dst, out_sems.at[12 + len(stores)])
+        copy.start()
+        stores.append(copy)
+
+    def store_sum(grads, ref, lead):
+        for part, rows in grads.summed():
+            store(part, ref.at[lead, rows])
+
+    stored = []
+
+    def stored_all():
+        for copy in stores[len(stored) :]:
+            copy.wait()
+            stored.append(copy)
+
+    def step0(block):
+        if block:
+            may(0)
+        ups[block].core_send()
+        downs[block].core_send()
+
+    def step1(block):
+        ups[block].core_add()
+        downs[block].core_add()
+        if block < BLOCKS - 1:
+            free(0, place.over_core)
+        if block:
+            may(1)
+            may(2)
+        ups[block].y_send()
+        downs[block].x_send()
+
+    def step2(block):
+        ups[block].y_add()
+        downs[block].x_add()
+        if block < BLOCKS - 1:
+            free(1, place.over_y)
+            free(2, place.over_x)
+        if block:
+            may(3)
+            may(4)
+        ups[block].x_send()
+        downs[block].y_send()
+
+    def step3(block):
+        ups[block].x_add()
+        downs[block].y_add()
+        if block < BLOCKS - 1:
+            free(3, place.over_x)
+            free(4, place.over_y)
+        stored_all()
+        ups[block].rs_send()
+        downs[block].rs_send()
+
+    def step4(block):
+        ups[block].rs_add()
+        downs[block].rs_add()
+        ups[block].ag_send()
+        downs[block].ag_send()
+
+    def step5(block):
+        ups[block].ag_wait()
+        downs[block].ag_wait()
+        store_sum(ups[block], gup, block)
+        store_sum(downs[block], gdown, block)
 
     hooks = {
         (0, 0): [pieces[7].second, pieces[6].third],
@@ -419,6 +760,18 @@
         (1, 0): [pieces[9].second, pieces[8].third],
         (1, 1): [pieces[9].third],
     }
+    if split:
+        hooks.update(
+            {
+                (1, 2): [lambda: step0(0)],
+                (2, 0): [lambda: step1(0)],
+                (3, 0): [lambda: step2(0)],
+                (3, 2): [lambda: step0(1)],
+                (4, 0): [lambda: step3(0), lambda: step1(1)],
+                (5, 0): [lambda: step4(0), lambda: step2(1)],
+                (5, 2): [lambda: step0(2)],
+            }
+        )
     for order in range(2 * BLOCKS):
         half, block = order % 2, order // 2
         index = half * BLOCKS + block
@@ -437,7 +790,7 @@
             act_grad[rows, :] = low
             return carry + jnp.sum(low.astype(F32), axis=0, keepdims=True)
 
-        up_sum[index : index + 1, :] = lax.fori_loop(
+        sums[2 * half, 2 + block : 3 + block, :512] = lax.fori_loop(
             0, QUAD, hidden, jnp.zeros((1, 512), F32)
         )
         for step in hooks.get((order, 0), ()):
@@ -464,13 +817,12 @@
             pieces[5 + 2 * block].hop_y.wait_send()
         wup[index] = gup_now
         wdown[index] = gdown_now
-
-    copies = [
-        pltpu.make_async_copy(wup, gup, out_sems.at[0]),
-        pltpu.make_async_copy(wdown, gdown, out_sems.at[1]),
-    ]
-    for copy in copies:
-        copy.start()
+        for step in hooks.get((order, 2), ()):
+            step()
+
+    if not split:
+        store(wup, gup)
+        store(wdown, gdown)
 
     def ship(group):
         slot = lax.rem(group, 2)
@@ -492,14 +844,18 @@
         grad = gm[rows, :].astype(F32) + back
         acc_g[rows, :] = grad
         gm[rows, :] = grad.astype(BF16)
-        vectors[2:3, :] += jnp.sum(grad, axis=0, keepdims=True)
-        vectors[3:4, :] += gain_grad
-        vectors[4:5, :] += shift_grad
+        sums[1, 2:3, :] += jnp.sum(grad, axis=0, keepdims=True)
+        sums[1, 3:4, :] += gain_grad
+        sums[1, 4:5, :] += shift_grad
         return carry
 
     lax.fori_loop(0, QUAD, finish, 0)
     for group in (QUAD - 2, QUAD - 1):
         ship(jnp.int32(group)).wait()
+    if split:
+        step5(0)
+        step3(1)
+        step1(2)
 
     out_grad = h2
     for half in range(2):
@@ -509,28 +865,60 @@
     for half in range(2):
         cols = slice(384 * half, 384 * (half + 1))
         wout[half] = dot(att[:, cols], gm[...], TN).astype(BF16)
-    copies.append(pltpu.make_async_copy(wout, gout, out_sems.at[4]))
-    copies[-1].start()
-    copies[0].wait()
-
-    for half in (1, 0):
-        attend_back(qkv, half, out_grad, probs, scale, (0, 16))
+    if split:
+        outs.core_send()
+        free(5, place.over_core)
+        free(6, place.over_x)
+        free(7, place.over_y)
+        for device in place.over_z:
+            free(8, device)
+    else:
+        store(wout, gout)
+
+    def qkv_grads(half):
         for part in range(3):
             cols = slice(384 * part, 384 * (part + 1))
             grads = qkv[half, :, cols]
-            wup[3 * half + part, :, :384] = dot(h1[...], grads, TN).astype(BF16)
+            home, col = homes[half][part]
+            home[:width, col : col + 384] = dot(h1[...], grads, TN).astype(BF16)
             if part != 1:
-                at = 2 * half + part // 2
-                qv_sum[at : at + 1, :] = jnp.sum(grads.astype(F32), axis=0, keepdims=True)
-            index = 5 + 3 * half + part
-            copies.append(
-                pltpu.make_async_copy(
-                    wup.at[3 * half + part, :, pl.ds(0, 384)],
-                    gqkv.at[half, part],
-                    out_sems.at[index],
+                at = part // 2
+                sums[2 * half, at : at + 1, :half_width] = jnp.sum(
+                    grads.astype(F32), axis=0, keepdims=True
                 )
-            )
-            copies[-1].start()
+            if not split:
+                store(home.at[pl.ds(0, width), pl.ds(col, 384)], gqkv.at[half, part])
+
+    attend_back(qkv, 1, out_grad, probs, scale, (0, 8))
+    if split:
+        outs.core_add()
+        outs.y_send()
+        step4(1)
+        step2(2)
+    attend_back(qkv, 1, out_grad, probs, scale, (8, 16))
+    qkv_grads(1)
+    if split:
+        may(5)
+        for grads in qkvs:
+            grads.core_send((1,))
+        outs.y_add()
+        outs.x_send()
+        step5(1)
+        step3(2)
+    attend_back(qkv, 0, out_grad, probs, scale, (0, 8))
+    if split:
+        may(6)
+        for grads in qkvs:
+            grads.core_add((1,))
+            grads.x_send((1,))
+        outs.x_add()
+        outs.whole_send()
+    attend_back(qkv, 0, out_grad, probs, scale, (8, 16))
+    qkv_grads(0)
+    if split:
+        for grads in qkvs:
+            grads.core_send((0,))
+        step4(2)
 
     def last_norm(group, carry):
         rows = rows_of(group, quarter)
@@ -543,47 +931,110 @@
         values = x_rows[rows, :].astype(F32)
         back, gain_grad, shift_grad = norm_back(grad, values, gain1)
         acc_g[rows, :] += back
-        vectors[0:1, :] += gain_grad
-        vectors[1:2, :] += shift_grad
+        sums[1, 0:1, :] += gain_grad
+        sums[1, 1:2, :] += shift_grad
         return carry
 
-    lax.fori_loop(0, QUAD, last_norm, 0)
-    copies.append(pltpu.make_async_copy(acc_g, tokens_grad, out_sems.at[11]))
-    copies[-1].start()
-    for copy in copies[1:]:
-        copy.wait()
+    lax.fori_loop(0, QUAD // 2, last_norm, 0)
+    if split:
+        may(7)
+        for grads in qkvs:
+            grads.x_add((1,))
+            grads.y_send()
+        for grads in qkvs:
+            grads.core_add((0,))
+            grads.x_send((0,))
+    lax.fori_loop(QUAD // 2, QUAD, last_norm, 0)
+    store(acc_g, tokens_grad)
+    if split:
+        def small(src, dst, kind, device):
+            return pltpu.make_async_remote_copy(
+                src_ref=src,
+                dst_ref=dst,
+                send_sem=small_send.at[kind],
+                recv_sem=small_recv.at[kind],
+                device_id=device,
+                device_id_type=MESH,
+            )
+
+        kept = sums.at[pl.ds(0, 2)]
+        over_y = small(sums.at[pl.ds(1, 2)], sums_in.at[0], 0, place.over_y)
+        over_core = small(kept, sums_in.at[1], 1, place.over_core)
+        over_x = small(kept, sums_in.at[2], 2, place.over_x)
+        over_z = [
+            small(kept, sums_in.at[3 + k], 3 + k, device) for k, device in enumerate(place.over_z)
+        ]
+        over_y.start()
+        outs.whole_add()
+        store(outs.mine(), gout)
+        step5(2)
+        over_y.wait()
+        sums[0] += sums_in[0, 1]
+        sums[1] += sums_in[0, 0]
+        over_core.start()
+        may(8, 3)
+        over_core.wait()
+        sums[0:2] += sums_in[1]
+        over_x.start()
+        over_x.wait()
+        sums[0:2] += sums_in[2]
+        for copy in over_z:
+            copy.start()
+        for grads in qkvs:
+            grads.x_add((0,))
+            grads.y_add()
+            grads.rs_send()
+        for copy in over_z:
+            copy.wait()
+        sums[0:2] += sums_in[3] + sums_in[4] + sums_in[5]
+        for grads in qkvs:
+            grads.rs_add()
+            grads.ag_send()
+        for part, grads in enumerate(qkvs):
+            grads.ag_wait()
+            store_sum(grads, gqkv, part)
+    stored_all()
     for gather in pieces[:3]:
         gather.sent()
 
 
 def run_layer(split, *operands):
     tokens, qkv_weight = operands[1], operands[11]
-    slots, images, width = tokens.shape
+    images, width = operands[0].shape[1], tokens.shape[1]
     total = images * SLOT
     half = qkv_weight.shape[2]
     vmem = pl.BlockSpec(memory_space=pltpu.VMEM)
     anywhere = pl.BlockSpec(memory_space=pl.ANY)
     shape = jax.ShapeDtypeStruct
+    if split:
+        grads = [
+            shape((3, width // 4, half), BF16),
+            shape((half // 4, width), BF16),
+            shape((BLOCKS, width // 4, 512), BF16),
+            shape((BLOCKS, 128, width), BF16),
+        ]
+    else:
+        grads = [
+            shape((2, 3, width, half), BF16),
+            shape((2, half, width), BF16),
+            shape((2 * BLOCKS, width, 512), BF16),
+            shape((2 * BLOCKS, 512, width), BF16),
+        ]
     return pl.pallas_call(
         functools.partial(layer_kernel, split),
         out_shape=[
             shape((total, width), BF16),
             shape((total, width), F32),
-            shape((2, 3, width, half), BF16),
-            shape((2, half, width), BF16),
-            shape((2 * BLOCKS, width, 512), BF16),
-            shape((2 * BLOCKS, 512, width), BF16),
-            shape((8, width), F32),
-            shape((4, half), F32),
-            shape((2 * BLOCKS, 512), F32),
+            *grads,
+            shape((3, 8, width), F32),
         ],
         in_specs=[pl.BlockSpec(memory_space=pltpu.SMEM)]
         + [anywhere] * 2
         + [vmem] * 8
         + [anywhere] * 4,
-        out_specs=[anywhere] * 6 + [vmem] * 3,
+        out_specs=[anywhere] * 6 + [vmem],
         scratch_shapes=[
-            pltpu.VMEM((SLOT, images, width), BF16),
+            pltpu.VMEM((total, width), BF16),
             pltpu.VMEM((2, 3, width, half), BF16),
             pltpu.VMEM((2, half, width), BF16),
             pltpu.VMEM((2 * BLOCKS, width, 512), BF16),
@@ -603,9 +1054,24 @@
             pltpu.VMEM((total, 512), BF16),
             pltpu.VMEM((2, total // QUAD, width), BF16),
             pltpu.SemaphoreType.DMA((3 + 8 * BLOCKS,)),
-            pltpu.SemaphoreType.DMA((12,)),
+            pltpu.SemaphoreType.DMA((54,)),
             pltpu.SemaphoreType.DMA((11, 4)),
             pltpu.SemaphoreType.DMA((11, 4)),
+            pltpu.VMEM((2, 2, 192, 512), BF16),
+            pltpu.VMEM((2, 2, 128, width), BF16),
+            pltpu.VMEM((2, 192, 512), BF16),
+            pltpu.VMEM((2, 128, width), BF16),
+            pltpu.VMEM((192, 512), BF16),
+            pltpu.VMEM((128, width), BF16),
+            pltpu.VMEM((6, 48, 512), BF16),
+            pltpu.VMEM((6, 32, width), BF16),
+            pltpu.VMEM((10, 96, width), BF16),
+            pltpu.VMEM((6, 2, 8, width), F32),
+            pltpu.SemaphoreType.DMA((6, 14)),
+            pltpu.SemaphoreType.DMA((6, 14)),
+            pltpu.SemaphoreType.DMA((6,)),
+            pltpu.SemaphoreType.DMA((6,)),
+            pltpu.SemaphoreType.REGULAR((9,)),
         ],
         compiler_params=pltpu.CompilerParams(
             collective_id=0, has_side_effects=True, vmem_limit_bytes=64 * 2**20 - 2**17
@@ -634,11 +1100,13 @@
     inner = lax.axis_size("inner")
     head_width = qkv_weight.shape[2]
     hidden = up_weight.shape[1]
-    mixed, tokens_grad, gqkv, gout, gup, gdown, vectors, qv_sum, up_sum = run_layer(
-        inner == 4,
+    split = inner == 4 and lax.axis_size("outer") == 4
+    place = lax.axis_index("inner")
+    mixed, tokens_grad, gqkv, gout, gup, gdown, sums = run_layer(
+        split,
         counts,
-        tokens.transpose(1, 0, 2),
-        cotangent.transpose(1, 0, 2),
+        tokens.transpose(1, 0, 2).reshape(slots * images, width),
+        cotangent.transpose(1, 0, 2).reshape(slots * images, width),
         norm1_gain,
         norm1_shift,
         out_bias,
@@ -654,48 +1122,56 @@
     )
     mixed = mixed.reshape(images, SLOT, width)[:, :slots]
     tokens_grad = tokens_grad.reshape(images, SLOT, width)[:, :slots]
-
-    def own_half(grads):
-        other = lax.ppermute(grads[1].astype(BF16), "tensor", [(0, 1), (1, 0)])
-        return (grads[0].astype(F32) + other.astype(F32)).astype(BF16)
-
-    gqkv = own_half(gqkv).transpose(1, 0, 2)
-    gout = own_half(gout)
-    back = lambda v: v.reshape(BLOCKS, width, 4, 128).transpose(1, 2, 0, 3).reshape(width, hidden)
-    gup = back(own_half(gup.reshape(2, BLOCKS, width, 512)))
-    gdown = own_half(gdown.reshape(2, BLOCKS, 512, width))
-    gdown = gdown.reshape(BLOCKS, 4, 128, width).transpose(1, 0, 2, 3).reshape(hidden, width)
-    qv_sum = own_half(qv_sum.reshape(2, 2, head_width))
-    up_sum = own_half(up_sum.reshape(2, BLOCKS, 512))
-    up_sum = up_sum.reshape(BLOCKS, 4, 128).transpose(1, 0, 2).reshape(hidden)
-    vectors = lax.psum(vectors.astype(BF16), "tensor")
-
-    def reduce(grads, dim=0):
-        part = lax.psum_scatter(grads, "inner", scatter_dimension=dim, tiled=True)
-        return lax.psum(part, "outer").astype(F32)
-
-    gqkv = reduce(gqkv)
-    gout = reduce(gout)
-    gup = reduce(gup)
-    gdown = reduce(gdown)
-    vectors = reduce(vectors.T)
-    qv_sum = reduce(qv_sum.T).T
-    up_sum = reduce(up_sum)
+    if split:
+        gqkv = gqkv.transpose(1, 0, 2).astype(F32)
+        gout = gout.astype(F32)
+        gup = gup.reshape(BLOCKS, width // inner, 4, 128).transpose(1, 2, 0, 3)
+        gup = gup.reshape(width // inner, hidden).astype(F32)
+        gdown = gdown.reshape(hidden // inner, width).astype(F32)
+        cut = width // inner
+        shared = lax.dynamic_slice(sums[1], (0, place * cut), (6, cut))
+        vectors = [shared[k] for k in range(6)]
+        cut = head_width // inner
+        qv_sum = lax.dynamic_slice(sums[0], (0, place * cut), (2, cut))
+        up_sum = lax.dynamic_slice(sums[0], (2, place * 128), (BLOCKS, 128)).reshape(-1)
+    else:
+
+        def own_half(first, second):
+            other = lax.ppermute(second.astype(BF16), "tensor", [(0, 1), (1, 0)])
+            return (first.astype(F32) + other.astype(F32)).astype(BF16)
+
+        def reduce(grads, dim=0):
+            part = lax.psum_scatter(grads, "inner", scatter_dimension=dim, tiled=True)
+            return lax.psum(part, "outer").astype(F32)
+
+        gqkv = reduce(own_half(*gqkv).transpose(1, 0, 2))
+        gout = reduce(own_half(*gout))
+        gup = own_half(gup[:BLOCKS], gup[BLOCKS:])
+        gup = gup.reshape(BLOCKS, width, 4, 128).transpose(1, 2, 0, 3).reshape(width, hidden)
+        gup = reduce(gup)
+        gdown = own_half(gdown[:BLOCKS], gdown[BLOCKS:])
+        gdown = gdown.reshape(BLOCKS, 4, 128, width).transpose(1, 0, 2, 3)
+        gdown = reduce(gdown.reshape(hidden, width))
+        own = own_half(sums[0], sums[2])
+        qv_sum = reduce(own[:2, :head_width].T).T
+        up_sum = own[2 : 2 + BLOCKS, :512].reshape(BLOCKS, 4, 128).transpose(1, 0, 2)
+        up_sum = reduce(up_sum.reshape(hidden))
+        vectors = reduce(lax.psum(sums[1].astype(BF16), "tensor").T).T
     return (
         mixed,
         tokens_grad,
-        vectors[:, 0],
-        vectors[:, 1],
+        vectors[0],
+        vectors[1],
         gqkv,
         qv_sum,
         gout,
-        vectors[:, 2],
-        vectors[:, 3],
-        vectors[:, 4],
+        vectors[2],
+        vectors[3],
+        vectors[4],
         gup,
         up_sum,
         gdown,
-        vectors[:, 5],
+        vectors[5],
     )
 
 

time: 505 us -> 214 us (0.42)
  waiting for transfers between devices: 265 us -> 0 us
  Pallas kernels: 144 us -> 192 us
  blocking collectives: 23.3 us -> 0 us
  local copies, waits for them, and re-layouts: 35 us -> 14.3 us
  between operations: 15.5 us -> 0.92 us
  other arithmetic: 11.9 us -> 2.83 us
  starting transfers between devices: 5.73 us -> 0 us
    ppermute x6 -> x0, waiting for transfers between devices: 144 us -> none  [own_half(): other = lax.ppermute(grads[1].astype(BF16), 'tensor', [(0, 1), (1, 0)])]
    psum x1 -> x0, waiting for transfers between devices: 66.8 us -> none  [reduce(): return lax.psum(part, 'outer').astype(F32)]
    pallas_call x1, Pallas kernels: 144 us -> 192 us  [run_layer(): pl.pallas_call(functools.partial(layer_kernel, split), out_shape=[shape((...]
    unnamed x10 -> x0, waiting for transfers between devices: 27.7 us -> none
    reduce_scatter x3 -> x0, waiting for transfers between devices: 26 us -> none  [reduce(): part = lax.psum_scatter(grads, 'inner', scatter_dimension=dim, tiled=True)]
    psum x2 -> x0, blocking collectives: 17.3 us -> none  [the longest x1 12.4 us: reduce(): return lax.psum(part, 'outer').astype(F32)]
    unnamed x31 -> x12, local copies, waits for them, and re-layouts: 19.7 us -> 9.68 us
    unnamed x1 -> x0, blocking collectives: 5.96 us -> none
  transfers between devices with their start and end apart: 13 -> 0, of which waited for: 8 -> 0; matrix products, arithmetic and copies ran while one was open for 6% -> 0% of each run, Pallas kernels for 0% -> 0%
where the time goes in v3:
time: 214 us; the launch traced here: 210 us
  Pallas kernels  192 us (90%)
  local copies, waits for them, and re-layouts  14.3 us (7%)
  other arithmetic  2.83 us (1%)
    pallas_call x1, Pallas kernels, run_layer(): pl.pallas_call(functools.partial(layer_kernel, split), out_shape=[shape((...  192 us
    unnamed x12, local copies, waits for them, and re-layouts  9.68 us

profile of v3, /device:TPU:0, one launch (start us, length us, event | category | flops | bytes accessed | tf_op | source)
XLA Modules:
  0.0 209.9 jit_solution(2996895396012859054)
XLA Ops:
  0.7 191.9 %shard_map.254 = (bf16[1280,768]{1,0:T(8,128)(2,1)}, f32[1280,768]{1,0:T(8,128)}, bf16[3,192,384]{2,1,0:T(8,128)(2,1)}, bf16[96,768]{1,0:T(8,128)(2,1)}, bf16[3,...) custom-call(s32[2,16]{1,0:T(2,128)} %counts.1, bf16[1248,768]{1,0:T(8,128)(2,1)} %bitcast.32, ...), custom_call_target="tpu_custom_call" | custom-call | tf_op jit(solution)/shard_map/pallas_call | solution.py:1023
  192.6 3.4 %copy.35 = bf16[16,78,768]{2,0,1:T(8,128)(2,1)} copy(bf16[16,78,768]{2,1,0:T(8,128)(2,1)} %bitcast.31) | data formatting | bytes 3833856
  195.9 0.0 copy-start.4
  195.9 0.0 copy-start.2
  195.9 0.0 copy-start.3
  195.9 6.3 %copy.36 = f32[16,78,768]{2,0,1:T(8,128)} copy(f32[16,78,768]{2,1,0:T(8,128)} %bitcast.30) | data formatting | bytes 7667712
  202.2 0.0 copy-start.1
  202.2 0.0 copy-done.4
  202.2 0.7 constant_dynamic-slice_fusion.6
  202.9 0.0 copy-done.2
  202.9 1.0 convert_bitcast_fusion
  203.9 0.6 fusion
  204.5 0.0 copy-done.3
  204.5 0.7 convert_element_type.29
  205.3 0.0 copy-done.1
  205.3 0.4 reshape.75
  205.6 0.8 copy.38
  206.4 0.0 copy-start
  206.5 1.5 reshape.73
  207.9 0.7 dynamic-slice_bitcast_fusion
  208.6 0.0 copy-done
  208.6 1.1 bitcast_convert_fusion
  (1 shorter events, 0.0 us)
Async XLA Ops:
  195.9 6.3 %copy-start.4 = (f32[3,8,768]{2,1,0:T(8,128)S(1)}, f32[3,8,768]{2,1,0:T(8,128)}, u32[]{:S(2)}) copy-start(f32[3,8,768]{2,1,0:T(8,128)} %get-tuple-element.23) | copy-start | bytes 221188
  195.9 7.0 %copy-start.2 = (bf16[3,192,384]{2,1,0:T(8,128)(2,1)S(1)}, bf16[3,192,384]{2,1,0:T(8,128)(2,1)}, u32[]{:S(2)}) copy-start(bf16[3,192,384]{2,1,0:T(8,128)(2,1)} %get-tuple-element.24) | copy-start | bytes 1327108
  195.9 8.6 %copy-start.3 = (bf16[96,768]{1,0:T(8,128)(2,1)S(1)}, bf16[96,768]{1,0:T(8,128)(2,1)}, u32[]{:S(2)}) copy-start(bf16[96,768]{1,0:T(8,128)(2,1)} %get-tuple-element.25) | copy-start | bytes 442372
  202.2 3.0 %copy-start.1 = (bf16[3,192,512]{2,1,0:T(8,128)(2,1)S(1)}, bf16[3,192,512]{2,1,0:T(8,128)(2,1)}, u32[]{:S(2)}) copy-start(bf16[3,192,512]{2,1,0:T(8,128)(2,1)} %get-tuple-element.26) | copy-start | bytes 1769476
  206.4 2.1 %copy-start = (bf16[3,128,768]{2,1,0:T(8,128)(2,1)S(1)}, bf16[3,128,768]{2,1,0:T(8,128)(2,1)}, u32[]{:S(2)}) copy-start(bf16[3,128,768]{2,1,0:T(8,128)(2,1)} %get-tuple-element.27) | copy-start | bytes 1769476

commit v4 on v3

--- a/solution.py
+++ b/solution.py
@@ -351,12 +351,10 @@
         self.mine()[...] = total.astype(BF16)
 
 
-def row_part(ref, lead, total, count):
+def row_part(ref, lead, total, count, cols=None):
     def part(index, whole):
-        if whole:
-            return ref.at[(*lead, pl.ds(0, total))]
-        size = total // count
-        return ref.at[(*lead, rows_of(index, size))]
+        rows = pl.ds(0, total) if whole else rows_of(index, total // count)
+        return ref.at[(*lead, rows) if cols is None else (*lead, rows, cols)]
 
     return part
 
@@ -403,7 +401,6 @@
     acc_g,
     act,
     act_grad,
-    mixed_part,
     sems,
     out_sems,
     send,
@@ -441,9 +438,16 @@
 
     loads = [
         pltpu.make_async_copy(tokens, staged.at[pl.ds(0, slots * images)], sems.at[0]),
-        pltpu.make_async_copy(qkv_weight, wqkv.at[0], sems.at[1]),
-        pltpu.make_async_copy(out_weight, wout.at[0], sems.at[2]),
+        pltpu.make_async_copy(out_weight, wout.at[0], sems.at[1]),
     ]
+    for part in range(3):
+        loads.append(
+            pltpu.make_async_copy(
+                qkv_weight.at[part],
+                wqkv.at[0, :, pl.ds(part * half_width, half_width)],
+                sems.at[2 + part],
+            )
+        )
     for block in range(BLOCKS):
         for q in range(4):
             at = q * 384 + block * 128
@@ -461,7 +465,7 @@
                     sems.at[len(loads)],
                 )
             )
-    for load in loads:
+    for load in loads[:5]:
         load.start()
     pieces = []
 
@@ -470,23 +474,25 @@
         pieces.append(Gather(own, other, place, send.at[index], recv.at[index]))
 
     for part in range(3):
+        cols = pl.ds(part * half_width, half_width)
         piece(
-            row_part(qkv_weight, (part,), width, 4), row_part(wqkv, (1, part), width, 4)
+            row_part(qkv_weight, (part,), width, 4), row_part(wqkv, (1,), width, 4, cols)
         )
     piece(row_part(out_weight, (), half_width, 4), row_part(wout, (1,), half_width, 4))
     for block in range(BLOCKS):
         piece(row_part(wup, (block,), width, 4), row_part(wup, (BLOCKS + block,), width, 4))
         piece(row_part(wdown, (block,), 512, 4), row_part(wdown, (BLOCKS + block,), 512, 4))
-    biases[...] = jnp.zeros_like(biases)
+    place.meet()
+    for gather in pieces[:4]:
+        gather.first()
+    biases[0] = jnp.zeros(biases.shape[1:], F32)
     for block in range(BLOCKS):
         for q in range(4):
             at = q * 384 + block * 128
             found = up_bias[pl.ds(at, 128)].reshape(1, 128)
             biases[0, block : block + 1, q * 128 : (q + 1) * 128] = found
-    biases[0, 3:5, :half_width] = qv_bias[...]
-    place.meet()
-    for gather in pieces[:4]:
-        gather.first()
+    biases[0, 3:4, :half_width] = qv_bias[0:1, :]
+    biases[0, 3:4, 2 * half_width :] = qv_bias[1:2, :]
     bias_copy = pltpu.make_async_remote_copy(
         src_ref=biases.at[0],
         dst_ref=biases.at[1],
@@ -516,6 +522,8 @@
         lax.fori_loop(0, SLOT // 16, some_slots, 0)
 
     loads[0].wait()
+    for load in loads[5:]:
+        load.start()
     by_image(x_rows, False)
     load = pltpu.make_async_copy(cotangent, staged.at[pl.ds(0, slots * images)], sems.at[0])
     load.start()
@@ -532,49 +540,56 @@
         return carry
 
     lax.fori_loop(0, QUAD, first_norm, 0)
-    for later in loads[1:]:
+    for later in loads[1:5]:
+        later.wait()
+    pieces[0].second()
+
+    def project(half, start, stop):
+        cols = slice(start, stop)
+        found = dot(h1[...], wqkv[half, :, cols], NN) + biases[half, 3:4, cols]
+        qkv[half, :, cols] = found.astype(BF16)
+
+    project(0, 0, 512)
+    project(0, 512, 1024)
+    project(0, 1024, 1152)
+    pieces[1].second()
+    load.wait()
+    by_image(gm, True)
+    pieces[2].second()
+    pieces[0].third()
+    for later in loads[5:]:
         later.wait()
     for gather in pieces[4:]:
         gather.first()
-    pieces[0].second()
-
-    def project(half, part):
-        found = dot(h1[...], wqkv[half, part], NN)
-        if part != 1:
-            row = 3 + part // 2
-            found = found + biases[half, row : row + 1, :half_width]
-        qkv[half, :, 384 * part : 384 * (part + 1)] = found.astype(BF16)
-
-    for part in range(3):
-        project(0, part)
-    pieces[1].second()
     attend(count_of, qkv, 0, att, probs, scale, (0, 8))
-    pieces[2].second()
-    pieces[0].third()
-    load.wait()
-    by_image(gm, True)
     pieces[1].third()
     attend(count_of, qkv, 0, att, probs, scale, (8, 16))
+    pieces[2].third()
     pieces[3].second()
-    pieces[2].third()
     bias_copy.wait()
-    for part in range(3):
-        pieces[part].ready()
-        project(1, part)
+    pieces[0].ready()
+    pieces[1].ready()
+    project(1, 0, 512)
+    pieces[2].ready()
+    project(1, 512, 1024)
+    project(1, 1024, 1152)
     pieces[3].third()
     pieces[4].second()
     attend(count_of, qkv, 1, att, probs, scale, (0, 8))
     pieces[5].second()
-    pieces[4].third()
     attend(count_of, qkv, 1, att, probs, scale, (8, 16))
     pieces[3].ready()
-
-    for part in range(2):
-        cols = slice(384 * part, 384 * (part + 1))
-        weight = wout[:, :, cols].reshape(width, 384)
+    pieces[4].third()
+    pieces[6].second()
+
+    for part in range(3):
+        cols = slice(256 * part, 256 * (part + 1))
+        weight = wout[:, :, cols].reshape(width, 256)
         mid[:, cols] = (
             x_rows[:, cols].astype(F32) + dot(att[...], weight, NN) + out_bias[:, cols]
         )
+
+    pieces[5].third()
 
     def second_norm(group, carry):
         rows = rows_of(group, quarter)
@@ -584,8 +599,7 @@
         return carry
 
     lax.fori_loop(0, QUAD, second_norm, 0)
-    pieces[6].second()
-    pieces[5].third()
+    pieces[7].second()
 
     inner = place.at[1]
 
@@ -754,49 +768,45 @@
         store_sum(ups[block], gup, block)
         store_sum(downs[block], gdown, block)
 
-    hooks = {
-        (0, 0): [pieces[7].second, pieces[6].third],
-        (0, 1): [pieces[8].second, pieces[7].third],
-        (1, 0): [pieces[9].second, pieces[8].third],
-        (1, 1): [pieces[9].third],
-    }
+    hooks = [
+        [pieces[8].second, pieces[9].second, pieces[6].third, pieces[7].third],
+        [pieces[8].third, pieces[9].third],
+        [],
+        [],
+        [],
+        [],
+    ]
     if split:
-        hooks.update(
-            {
-                (1, 2): [lambda: step0(0)],
-                (2, 0): [lambda: step1(0)],
-                (3, 0): [lambda: step2(0)],
-                (3, 2): [lambda: step0(1)],
-                (4, 0): [lambda: step3(0), lambda: step1(1)],
-                (5, 0): [lambda: step4(0), lambda: step2(1)],
-                (5, 2): [lambda: step0(2)],
-            }
-        )
+        later = [
+            (1, [(step0, 0)]),
+            (2, [(step1, 0)]),
+            (3, [(step2, 0), (step0, 1)]),
+            (4, [(step3, 0), (step1, 1)]),
+            (5, [(step4, 0), (step2, 1), (step0, 2)]),
+        ]
+        for order, calls in later:
+            hooks[order] += [functools.partial(call, block) for call, block in calls]
     for order in range(2 * BLOCKS):
         half, block = order % 2, order // 2
         index = half * BLOCKS + block
-        bias = biases[half, block : block + 1, :]
+        bias = biases[half, block : block + 1, :512]
         if half == 1:
             pieces[4 + 2 * block].ready()
             pieces[5 + 2 * block].ready()
 
-        def hidden(group, carry, index=index, bias=bias):
-            rows = rows_of(group, quarter)
-            u = dot(h2[rows, :], wup[index], NN) + bias
+        for part in range(2):
+            cols = slice(256 * part, 256 * (part + 1))
+            u = dot(h2[...], wup[index, :, cols], NN) + bias[:, cols]
             cdf = 0.5 * (1.0 + lax.erf(u * 0.7071067811865476))
-            act[rows, :] = (u * cdf).astype(BF16)
+            act[:, cols] = (u * cdf).astype(BF16)
             slope = cdf + u * jnp.exp(-0.5 * u * u) * 0.3989422804014327
-            low = (dot(gm[rows, :], wdown[index], NT) * slope).astype(BF16)
-            act_grad[rows, :] = low
-            return carry + jnp.sum(low.astype(F32), axis=0, keepdims=True)
-
-        sums[2 * half, 2 + block : 3 + block, :512] = lax.fori_loop(
-            0, QUAD, hidden, jnp.zeros((1, 512), F32)
-        )
-        for step in hooks.get((order, 0), ()):
-            step()
-        for part in range(2):
-            cols = slice(384 * part, 384 * (part + 1))
+            low = (dot(gm[...], wdown[index, cols, :], NT) * slope).astype(BF16)
+            act_grad[:, cols] = low
+            sums[2 * half, 2 + block : 3 + block, cols] = jnp.sum(
+                low.astype(F32), axis=0, keepdims=True
+            )
+        for part in range(3):
+            cols = slice(256 * part, 256 * (part + 1))
             y = dot(act[...], wdown[index, :, cols], NN)
             g = dot(act_grad[...], wup[index, cols, :], NT)
             if order == 0:
@@ -805,8 +815,6 @@
             else:
                 acc_y[:, cols] += y
                 acc_g[:, cols] += g
-        for step in hooks.get((order, 1), ()):
-            step()
         if half == 1:
             pieces[4 + 2 * block].handed_on()
             pieces[5 + 2 * block].handed_on()
@@ -817,29 +825,18 @@
             pieces[5 + 2 * block].hop_y.wait_send()
         wup[index] = gup_now
         wdown[index] = gdown_now
-        for step in hooks.get((order, 2), ()):
+        for step in hooks[order]:
             step()
 
     if not split:
         store(wup, gup)
         store(wdown, gdown)
 
-    def ship(group):
-        slot = lax.rem(group, 2)
-        return pltpu.make_async_copy(
-            mixed_part.at[slot], mixed.at[rows_of(group, quarter)], out_sems.at[2 + slot]
-        )
-
     def finish(group, carry):
         rows = rows_of(group, quarter)
 
-        @pl.when(group >= 2)
-        def _():
-            ship(group - 2).wait()
-
         values = mid[rows, :]
-        mixed_part[lax.rem(group, 2)] = (values + acc_y[rows, :] + down_bias).astype(BF16)
-        ship(group).start()
+        acc_y[rows, :] += values + down_bias
         back, gain_grad, shift_grad = norm_back(acc_g[rows, :], values, gain2)
         grad = gm[rows, :].astype(F32) + back
         acc_g[rows, :] = grad
@@ -850,17 +847,16 @@
         return carry
 
     lax.fori_loop(0, QUAD, finish, 0)
-    for group in (QUAD - 2, QUAD - 1):
-        ship(jnp.int32(group)).wait()
     if split:
         step5(0)
         step3(1)
         step1(2)
 
     out_grad = h2
-    for half in range(2):
-        cols = slice(384 * half, 384 * (half + 1))
-        out_grad[:, cols] = dot(gm[...], wout[half], NT).astype(BF16)
+    for part in range(3):
+        cols = slice(256 * part, 256 * (part + 1))
+        weight = wout[...].reshape(width, width)[cols]
+        out_grad[:, cols] = dot(gm[...], weight, NT).astype(BF16)
     pieces[3].sent()
     for half in range(2):
         cols = slice(384 * half, 384 * (half + 1))
@@ -876,17 +872,20 @@
         store(wout, gout)
 
     def qkv_grads(half):
-        for part in range(3):
-            cols = slice(384 * part, 384 * (part + 1))
-            grads = qkv[half, :, cols]
-            home, col = homes[half][part]
-            home[:width, col : col + 384] = dot(h1[...], grads, TN).astype(BF16)
-            if part != 1:
-                at = part // 2
-                sums[2 * half, at : at + 1, :half_width] = jnp.sum(
-                    grads.astype(F32), axis=0, keepdims=True
-                )
-            if not split:
+        for start, stop in ((0, 512), (512, 1024), (1024, 1152)):
+            grads = qkv[half, :, start:stop]
+            found = dot(h1[...], grads, TN).astype(BF16)
+            for part in range(3):
+                low, high = max(start, 384 * part), min(stop, 384 * (part + 1))
+                if low < high:
+                    home, col = homes[half][part]
+                    at = col + low - 384 * part
+                    home[:width, at : at + high - low] = found[:, low - start : high - start]
+        for at in range(2):
+            grads = qkv[half, :, 768 * at : 768 * at + 384].astype(F32)
+            sums[2 * half, at : at + 1, :half_width] = jnp.sum(grads, axis=0, keepdims=True)
+        if not split:
+            for part, (home, col) in enumerate(homes[half]):
                 store(home.at[pl.ds(0, width), pl.ds(col, 384)], gqkv.at[half, part])
 
     attend_back(qkv, 1, out_grad, probs, scale, (0, 8))
@@ -922,12 +921,7 @@
 
     def last_norm(group, carry):
         rows = rows_of(group, quarter)
-        grad = None
-        for half in range(2):
-            for part in range(3):
-                cols = slice(384 * part, 384 * (part + 1))
-                term = dot(qkv[half, rows, cols], wqkv[half, part], NT)
-                grad = term if grad is None else grad + term
+        grad = dot(qkv[0, rows, :], wqkv[0], NT) + dot(qkv[1, rows, :], wqkv[1], NT)
         values = x_rows[rows, :].astype(F32)
         back, gain_grad, shift_grad = norm_back(grad, values, gain1)
         acc_g[rows, :] += back
@@ -945,7 +939,18 @@
             grads.core_add((0,))
             grads.x_send((0,))
     lax.fori_loop(QUAD // 2, QUAD, last_norm, 0)
-    store(acc_g, tokens_grad)
+    def by_slot(source, target):
+        def some_slots(step, carry):
+            parts = []
+            for image in range(images):
+                parts.append(source[pl.ds(pl.multiple_of(image * SLOT + step * 16, 16), 16), :])
+            values = jnp.concatenate(parts, axis=0).reshape(images, 16, width)
+            values = jnp.swapaxes(values, 0, 1).reshape(16 * images, width)
+            target[rows_of(step, 16 * images), :] = values.astype(target.dtype)
+            return carry
+
+        lax.fori_loop(0, SLOT // 16, some_slots, 0)
+
     if split:
         def small(src, dst, kind, device):
             return pltpu.make_async_remote_copy(
@@ -964,35 +969,50 @@
         over_z = [
             small(kept, sums_in.at[3 + k], 3 + k, device) for k, device in enumerate(place.over_z)
         ]
+
+        def qkv_rs(part):
+            qkvs[part].x_add((0,))
+            qkvs[part].y_add()
+            qkvs[part].rs_send()
+
         over_y.start()
-        outs.whole_add()
-        store(outs.mine(), gout)
-        step5(2)
+        may(8, 3)
+        qkv_rs(0)
         over_y.wait()
         sums[0] += sums_in[0, 1]
         sums[1] += sums_in[0, 0]
         over_core.start()
-        may(8, 3)
+        qkv_rs(1)
         over_core.wait()
         sums[0:2] += sums_in[1]
         over_x.start()
+        qkv_rs(2)
         over_x.wait()
         sums[0:2] += sums_in[2]
         for copy in over_z:
             copy.start()
+        outs.whole_add()
+        store(outs.mine(), gout)
+        step5(2)
+        by_slot(acc_y, x_rows)
+        store(x_rows.at[pl.ds(0, slots * images)], mixed)
         for grads in qkvs:
-            grads.x_add((0,))
-            grads.y_add()
-            grads.rs_send()
+            grads.rs_add()
+            grads.ag_send()
+        by_slot(acc_g, acc_y)
+        store(acc_y.at[pl.ds(0, slots * images)], tokens_grad)
         for copy in over_z:
             copy.wait()
         sums[0:2] += sums_in[3] + sums_in[4] + sums_in[5]
-        for grads in qkvs:
-            grads.rs_add()
-            grads.ag_send()
         for part, grads in enumerate(qkvs):
             grads.ag_wait()
             store_sum(grads, gqkv, part)
+    else:
+        by_slot(acc_y, x_rows)
+        store(x_rows.at[pl.ds(0, slots * images)], mixed)
+        stored_all()
+        by_slot(acc_g, acc_y)
+        store(acc_y.at[pl.ds(0, slots * images)], tokens_grad)
     stored_all()
     for gather in pieces[:3]:
         gather.sent()
@@ -1023,8 +1043,8 @@
     return pl.pallas_call(
         functools.partial(layer_kernel, split),
         out_shape=[
-            shape((total, width), BF16),
-            shape((total, width), F32),
+            shape(tokens.shape, BF16),
+            shape(tokens.shape, F32),
             *grads,
             shape((3, 8, width), F32),
         ],
@@ -1035,11 +1055,11 @@
         out_specs=[anywhere] * 6 + [vmem],
         scratch_shapes=[
             pltpu.VMEM((total, width), BF16),
-            pltpu.VMEM((2, 3, width, half), BF16),
+            pltpu.VMEM((2, width, 3 * half), BF16),
             pltpu.VMEM((2, half, width), BF16),
             pltpu.VMEM((2 * BLOCKS, width, 512), BF16),
             pltpu.VMEM((2 * BLOCKS, 512, width), BF16),
-            pltpu.VMEM((2, 8, 512), F32),
+            pltpu.VMEM((2, 8, 3 * half), F32),
             pltpu.VMEM((total, width), BF16),
             pltpu.VMEM((total, width), BF16),
             pltpu.VMEM((total, width), BF16),
@@ -1052,8 +1072,7 @@
             pltpu.VMEM((total, width), F32),
             pltpu.VMEM((total, 512), BF16),
             pltpu.VMEM((total, 512), BF16),
-            pltpu.VMEM((2, total // QUAD, width), BF16),
-            pltpu.SemaphoreType.DMA((3 + 8 * BLOCKS,)),
+            pltpu.SemaphoreType.DMA((5 + 8 * BLOCKS,)),
             pltpu.SemaphoreType.DMA((54,)),
             pltpu.SemaphoreType.DMA((11, 4)),
             pltpu.SemaphoreType.DMA((11, 4)),
@@ -1120,8 +1139,8 @@
         up_weight,
         down_weight,
     )
-    mixed = mixed.reshape(images, SLOT, width)[:, :slots]
-    tokens_grad = tokens_grad.reshape(images, SLOT, width)[:, :slots]
+    mixed = mixed.reshape(slots, images, width).transpose(1, 0, 2)
+    tokens_grad = tokens_grad.reshape(slots, images, width).transpose(1, 0, 2)
     if split:
         gqkv = gqkv.transpose(1, 0, 2).astype(F32)
         gout = gout.astype(F32)

time: 214 us -> 197 us (0.921)
  Pallas kernels: 192 us -> 176 us
  local copies, waits for them, and re-layouts: 14.3 us -> 10.1 us
  other arithmetic: 2.83 us -> 5.78 us
    pallas_call x1, Pallas kernels: 192 us -> 176 us  [run_layer(): pl.pallas_call(functools.partial(layer_kernel, split), out_shape=[shape(t...]
    unnamed x12 -> x8, local copies, waits for them, and re-layouts: 9.68 us -> 4.68 us
where the time goes in v4:
time: 197 us; the launch traced here: 193 us
  Pallas kernels  176 us (89%)
  local copies, waits for them, and re-layouts  10.1 us (5%)
  other arithmetic  5.78 us (3%)
    pallas_call x1, Pallas kernels, run_layer(): pl.pallas_call(functools.partial(layer_kernel, split), out_shape=[shape(t...  176 us
    unnamed x8, local copies, waits for them, and re-layouts  4.68 us

profile of v4, /device:TPU:0, one launch (start us, length us, event | category | flops | bytes accessed | tf_op | source)
XLA Modules:
  0.0 193.3 jit_solution(11705625930700101081)
XLA Ops:
  0.7 176.3 %shard_map.254 = (bf16[1248,768]{1,0:T(8,128)(2,1)}, f32[1248,768]{1,0:T(8,128)}, bf16[3,192,384]{2,1,0:T(8,128)(2,1)}, bf16[96,768]{1,0:T(8,128)(2,1)}, bf16[3,...) custom-call(s32[2,16]{1,0:T(2,128)} %counts.1, bf16[1248,768]{1,0:T(8,128)(2,1)} %bitcast.33, ...), custom_call_target="tpu_custom_call" | custom-call | tf_op jit(solution)/shard_map/pallas_call | solution.py:1043
  176.9 0.0 copy-start.2
  177.0 0.8 fusion.1
  177.8 0.7 constant_dynamic-slice_fusion.6
  178.4 2.0 %convert_bitcast_fusion = f32[192,3,384]{2,0,1:T(8,128)} fusion(bf16[3,192,384]{2,1,0:T(8,128)(2,1)} %get-tuple-element.24), kind=kLoop, calls=%fused_computation.1 | loop fusion | flops 221184 | bytes 1327104 | tf_op jit(solution)/shard_map/convert_element_type | solution.py:1145
  180.4 0.6 fusion
  181.1 1.6 convert_element_type.29
  182.7 0.0 copy-done.2
  182.7 0.4 reshape.75
  183.1 0.8 copy.32
  183.9 0.0 copy-start.1
  183.9 1.5 reshape.73
  185.4 0.7 dynamic-slice_bitcast_fusion
  186.0 2.2 %bitcast_convert_fusion = f32[384,768]{1,0:T(8,128)} fusion(bf16[3,128,768]{2,1,0:T(8,128)(2,1)} %get-tuple-element.27), kind=kLoop, calls=%fused_computation.2 | loop fusion | flops 294912 | bytes 1769472 | tf_op jit(solution)/shard_map/convert_element_type | solution.py:1149
  188.2 0.0 copy-done.1
  188.2 0.0 copy-start
  188.2 1.3 copy.35
  189.4 1.5 copy-done
  191.0 1.9 copy.36
Async XLA Ops:
  176.9 5.8 %copy-start.2 = (bf16[3,192,512]{2,1,0:T(8,128)(2,1)S(1)}, bf16[3,192,512]{2,1,0:T(8,128)(2,1)}, u32[]{:S(2)}) copy-start(bf16[3,192,512]{2,1,0:T(8,128)(2,1)} %get-tuple-element.26) | copy-start | bytes 1769476
  183.9 4.3 %copy-start.1 = (bf16[1248,768]{1,0:T(8,128)(2,1)S(1)}, bf16[1248,768]{1,0:T(8,128)(2,1)}, u32[]{:S(2)}) copy-start(bf16[1248,768]{1,0:T(8,128)(2,1)} %get-tuple-element.21) | copy-start | bytes 5750788
  188.2 2.8 %copy-start = (f32[1248,768]{1,0:T(8,128)S(1)}, f32[1248,768]{1,0:T(8,128)}, u32[]{:S(2)}) copy-start(f32[1248,768]{1,0:T(8,128)} %get-tuple-element.22) | copy-start | bytes 11501572

commit v5 on v4

--- a/solution.py
+++ b/solution.py
@@ -1098,6 +1098,72 @@
     )(*operands)
 
 
+def widen_kernel(
+    mixed,
+    tokens_grad,
+    gqkv,
+    gout,
+    gup,
+    gdown,
+    mixed_out,
+    tokens_out,
+    fqkv,
+    fout,
+    fup,
+    fdown,
+    held_mixed,
+    held_tokens,
+    sems,
+):
+    loads, stores = [], []
+    ways = ((mixed, held_mixed, mixed_out), (tokens_grad, held_tokens, tokens_out))
+    for source, held, target in ways:
+        size = source.shape[0] // 3
+        for part in range(3):
+            rows = pl.ds(part * size, size)
+            at = len(loads)
+            loads.append(pltpu.make_async_copy(source.at[rows], held.at[rows], sems.at[at]))
+            stores.append(pltpu.make_async_copy(held.at[rows], target.at[rows], sems.at[6 + at]))
+            loads[-1].start()
+    fqkv[...] = gqkv[...].astype(F32)
+    fout[...] = gout[...].astype(F32)
+    for load, store in zip(loads, stores):
+        load.wait()
+        store.start()
+    fdown[...] = gdown[...].astype(F32)
+    for block in range(BLOCKS):
+        for q in range(4):
+            at = q * 384 + block * 128
+            fup[:, at : at + 128] = gup[block, :, q * 128 : (q + 1) * 128].astype(F32)
+    for store in stores:
+        store.wait()
+
+
+def widen(mixed, tokens_grad, gqkv, gout, gup, gdown):
+    vmem = pl.BlockSpec(memory_space=pltpu.VMEM)
+    anywhere = pl.BlockSpec(memory_space=pl.ANY)
+    shape = jax.ShapeDtypeStruct
+    return pl.pallas_call(
+        widen_kernel,
+        out_shape=[
+            shape(mixed.shape, BF16),
+            shape(tokens_grad.shape, F32),
+            shape(gqkv.shape, F32),
+            shape(gout.shape, F32),
+            shape((gup.shape[1], BLOCKS * gup.shape[2]), F32),
+            shape(gdown.shape, F32),
+        ],
+        in_specs=[anywhere] * 2 + [vmem] * 4,
+        out_specs=[anywhere] * 2 + [vmem] * 4,
+        scratch_shapes=[
+            pltpu.VMEM(mixed.shape, BF16),
+            pltpu.VMEM(tokens_grad.shape, F32),
+            pltpu.SemaphoreType.DMA((12,)),
+        ],
+        compiler_params=pltpu.CompilerParams(vmem_limit_bytes=64 * 2**20 - 2**17),
+    )(mixed, tokens_grad, gqkv, gout, gup, gdown)
+
+
 def local(
     tokens,
     counts,
@@ -1139,14 +1205,15 @@
         up_weight,
         down_weight,
     )
+    if split:
+        mixed, tokens_grad, gqkv, gout, gup, gdown = widen(
+            mixed, tokens_grad, gqkv, gout, gup, gdown
+        )
     mixed = mixed.reshape(slots, images, width).transpose(1, 0, 2)
     tokens_grad = tokens_grad.reshape(slots, images, width).transpose(1, 0, 2)
     if split:
-        gqkv = gqkv.transpose(1, 0, 2).astype(F32)
-        gout = gout.astype(F32)
-        gup = gup.reshape(BLOCKS, width // inner, 4, 128).transpose(1, 2, 0, 3)
-        gup = gup.reshape(width // inner, hidden).astype(F32)
-        gdown = gdown.reshape(hidden // inner, width).astype(F32)
+        gqkv = gqkv.transpose(1, 0, 2)
+        gdown = gdown.reshape(hidden // inner, width)
         cut = width // inner
         shared = lax.dynamic_slice(sums[1], (0, place * cut), (6, cut))
         vectors = [shared[k] for k in range(6)]

time: 197 us -> 192 us (0.975)
  Pallas kernels: 176 us -> 185 us
  local copies, waits for them, and re-layouts: 10.1 us -> 2.7 us
  other arithmetic: 5.78 us -> 0 us
    pallas_call x0 -> x1, Pallas kernels: none -> 8.21 us  [widen(): pl.pallas_call(widen_kernel, out_shape=[shape(mixed.shape, BF16), shape(t...]
    convert_element_type x3 -> x0, other arithmetic: 5.78 us -> none  [the longest x1 2.15 us: local(): gdown = gdown.reshape(hidden // inner, width).astype(F32)]
    unnamed x8 -> x0, local copies, waits for them, and re-layouts: 4.68 us -> none
    convert_element_type x3 -> x0, local copies, waits for them, and re-layouts: 2.66 us -> none  [local(): gup = gup.reshape(width // inner, hidden).astype(F32)]
where the time goes in v5:
time: 192 us; the launch traced here: 189 us
  Pallas kernels  185 us (96%)
  local copies, waits for them, and re-layouts  2.7 us (1%)
    pallas_call x1, Pallas kernels, run_layer(): pl.pallas_call(functools.partial(layer_kernel, split), out_shape=[shape(t...  177 us
    pallas_call x1, Pallas kernels, widen(): pl.pallas_call(widen_kernel, out_shape=[shape(mixed.shape, BF16), shape(t...  8.21 us

profile of v5, /device:TPU:0, one launch (start us, length us, event | category | flops | bytes accessed | tf_op | source)
XLA Modules:
  0.0 188.8 jit_solution(12015225249793100277)
XLA Ops:
  0.7 177.0 %shard_map.254 = (bf16[1248,768]{1,0:T(8,128)(2,1)}, f32[1248,768]{1,0:T(8,128)}, bf16[3,192,384]{2,1,0:T(8,128)(2,1)}, bf16[96,768]{1,0:T(8,128)(2,1)}, bf16[3,...) custom-call(s32[2,16]{1,0:T(2,128)} %counts.1, bf16[1248,768]{1,0:T(8,128)(2,1)} %bitcast.25, ...), custom_call_target="tpu_custom_call" | custom-call | tf_op jit(solution)/shard_map/pallas_call | solution.py:1043
  177.6 0.8 fusion.1
  178.4 0.7 constant_dynamic-slice_fusion.6
  179.0 0.6 fusion
  179.7 0.7 dynamic-slice_bitcast_fusion
  180.3 8.2 %shard_map.255 = (bf16[1248,768]{1,0:T(8,128)(2,1)}, f32[1248,768]{1,0:T(8,128)}, f32[3,192,384]{2,1,0:T(8,128)}, f32[96,768]{1,0:T(8,128)}, f32[192,1536]{1,0:T(8,128)}, /*index=5*/f32[3,128,768]{2,1,0:T(8,128)}) custom-call(bf16[1248,768]{1,0:T(8,128)(2,1)} %get-tuple-element.27.mixed, f32[1248,768]{1,0:T(8,128)} %get-tuple-element.28.tokens_grad, ...), custom_call_target="tpu_custom_call" | custom-call | tf_op jit(solution)/shard_map/pallas_call | solution.py:1146
